TPU v7x, 128 devices: a whole 4x4x4 slice. The times are simulated.
128 devices in a mesh: seq: 32 (over x, y, core), head: 4 (over z).
Axes of the slice: x: 4, y: 4, z: 4, core: 2. Of those that a mesh axis runs over, the one named last changes fastest.
Arguments:
- clip_tokens: bfloat16 [4096, 5120], P(('seq', 'head')), may hold values from -11 to 11
- w_qkv: bfloat16 [3, 5120, 2560], P(None, None, 'head'), may hold values from -1 to 1
- readout: bfloat16 [4096, 2560], P('seq', 'head'), may hold values from -6 to 6
- token_latent_frame: int32 [4096], replicated, may hold values from 0 to 7, never falling along the last dimension, each value on 1 to 1024 neighbouring positions
- frame_mask: int32 [8, 8], replicated, may hold values from 0 to 1, as said below
Outputs:
- grad_x: bfloat16 [4096, 5120], P(('seq', 'head'))
- penalty_grad: bfloat16 [4096, 2560], P('seq', 'head')
Inputs may be any that keep to these rules, and one draw needn't show every extreme that they name: `token_latent_frame`: frames never fall along the tokens; each frame holds 1 to 1024 tokens, one exactly that many. `frame_mask`: entry (i, j) is 1 where tokens of frame i attend to tokens of frame j; it is 1 wherever i and j differ by at most one, and some farther pairs are 1 as well.
All inputs are finite; a program needn't handle non-finite values.
Results may differ from a plain program's by a relative error of at most 0.03.
The roundings to bfloat16 on the way count: a program that leaves them out, or rounds other values in their place, can miss the bound.
Values may be sent and summed in bfloat16 or wider, within the bound.
A program may use at most 192 MiB of HBM per device.

v0:
```python
import math

import jax
import jax.numpy as jnp
from jax import lax
from jax.sharding import PartitionSpec as P

HD = 128


masked_value = -1e30


def on_device(clip_tokens, w_qkv, readout, token_latent_frame, frame_mask):
    tok_rows = readout.shape[0]
    row_width = readout.shape[1]
    head_count = row_width // HD
    all_tokens = token_latent_frame.shape[0]
    frame_count = frame_mask.shape[0]
    score_scale = HD ** (-0.5)
    own_frames = lax.dynamic_slice_in_dim(
        token_latent_frame, lax.axis_index("seq") * tok_rows, tok_rows
    )
    mask_table = frame_mask.astype(jnp.float32)
    frame_ids = jnp.arange(frame_count, dtype=jnp.int32)

    def one_hot(ids):
        return (ids[..., None] == frame_ids).astype(jnp.float32)

    def allowed_for(reach_rows, key_ids):
        return jnp.einsum("...qf,kf->...qk", reach_rows, one_hot(key_ids)) > 0.5

    frame_reach = jnp.dot(one_hot(own_frames), mask_table)
    tokens_all = lax.all_gather(clip_tokens, "head", axis=0, tiled=True)
    projected = jnp.einsum(
        "td,cde->cte", tokens_all, w_qkv, preferred_element_type=jnp.float32
    ).astype(jnp.bfloat16)
    queries = projected[0]
    keys_own = projected[1]
    values_own = projected[2]
    keys_all, values_all = (
        lax.all_gather(keys_own, "seq", axis=0, tiled=True),
        lax.all_gather(values_own, "seq", axis=0, tiled=True),
    )
    query_heads = queries.reshape(tok_rows, head_count, HD)
    readout_heads = readout.reshape(tok_rows, head_count, HD)
    block_rows = math.gcd(all_tokens, 512)
    block_total = all_tokens // block_rows

    def blocked(array):
        return array.reshape(block_total, block_rows, head_count, HD)

    key_blocks = (
        blocked(keys_all),
        blocked(values_all),
        token_latent_frame.reshape(block_total, block_rows),
    )

    def dots_of(left_side, right_side):
        return jnp.einsum("qhd,khd->hqk", left_side, right_side, preferred_element_type=jnp.float32)

    def logits_of(allowed, left_side, right_side):
        return jnp.where(allowed[None], dots_of(left_side, right_side) * score_scale, masked_value)

    def stat_step(carry_in, key_block):
        block_keys, block_values, block_frames = key_block
        allowed = allowed_for(frame_reach, block_frames)
        row_max, row_sum, weighted = carry_in
        logits = logits_of(allowed, query_heads, block_keys)
        new_max = jnp.maximum(row_max, logits.max(-1))
        weights = jnp.where(allowed[None], jnp.exp(logits - new_max[..., None]), 0.0)
        rescale = jnp.exp(row_max - new_max)
        readout_dots = dots_of(readout_heads, block_values)
        return (
            (
                new_max,
                row_sum * rescale + weights.sum(-1),
                weighted * rescale + (weights * readout_dots).sum(-1),
            ),
            None,
        )

    stat_zero = jnp.zeros((head_count, tok_rows), jnp.float32)
    stat_init = (jnp.full((head_count, tok_rows), masked_value, jnp.float32), stat_zero, stat_zero)
    (row_max, row_sum, weighted), _ = lax.scan(stat_step, stat_init, key_blocks)
    log_norm = row_max + jnp.log(row_sum)
    row_dots = weighted / row_sum

    def probs_of(allowed, block_keys):
        logits = logits_of(allowed, query_heads, block_keys)
        return jnp.where(allowed[None], jnp.exp(logits - log_norm[..., None]), 0.0)

    zero_heads = jnp.zeros((tok_rows, head_count, HD), jnp.float32)

    def grad_step(carry_in, key_block):
        block_keys, block_values, block_frames = key_block
        allowed = allowed_for(frame_reach, block_frames)
        weights = probs_of(allowed, block_keys)
        logit_grads = (
            weights * (dots_of(readout_heads, block_values) - row_dots[..., None])
        ).astype(jnp.bfloat16)
        query_next = carry_in + score_scale * jnp.einsum(
            "hqk,khd->qhd", logit_grads, block_keys, preferred_element_type=jnp.float32
        )
        key_part = score_scale * jnp.einsum(
            "hqk,qhd->khd", logit_grads, query_heads, preferred_element_type=jnp.float32
        )
        value_part = jnp.einsum(
            "hqk,qhd->khd",
            weights.astype(jnp.bfloat16),
            readout_heads,
            preferred_element_type=jnp.float32,
        )
        return (query_next, (key_part, value_part))

    query_grad, (key_parts, value_parts) = lax.scan(grad_step, zero_heads, key_blocks)
    key_grad, value_grad = (
        lax.psum_scatter(
            key_parts.reshape(all_tokens, row_width).astype(jnp.bfloat16),
            "seq",
            scatter_dimension=0,
            tiled=True,
        ).astype(jnp.float32),
        lax.psum_scatter(
            value_parts.reshape(all_tokens, row_width).astype(jnp.bfloat16),
            "seq",
            scatter_dimension=0,
            tiled=True,
        ).astype(jnp.float32),
    )
    grads = jnp.stack([query_grad.reshape(tok_rows, row_width), key_grad, value_grad]).astype(
        jnp.bfloat16
    )
    partial_input = jnp.einsum("cte,cde->td", grads, w_qkv, preferred_element_type=jnp.float32)
    input_sum = lax.psum(partial_input.astype(jnp.bfloat16), "head")
    panel_rows = tok_rows // lax.axis_size("head")
    grad_x = lax.dynamic_slice_in_dim(input_sum, lax.axis_index("head") * panel_rows, panel_rows)
    tangents = jnp.einsum(
        "td,cde->cte", input_sum, w_qkv, preferred_element_type=jnp.float32
    ).astype(jnp.bfloat16)
    tangent_queries = tangents[0].reshape(tok_rows, head_count, HD)
    tangent_init = (zero_heads, zero_heads, jnp.zeros((head_count, tok_rows), jnp.float32))
    key_tangent = lax.all_gather(tangents[1], "seq", axis=0, tiled=True)
    value_tangent = lax.all_gather(tangents[2], "seq", axis=0, tiled=True)
    piece_rows = key_tangent.shape[0]
    sub_rows = math.gcd(piece_rows, 512)
    sub_count = piece_rows // sub_rows

    def to_blocks(array):
        return array.reshape(sub_count, sub_rows, head_count, HD)

    sub_blocks = (
        to_blocks(keys_all),
        to_blocks(values_all),
        to_blocks(key_tangent),
        to_blocks(value_tangent),
        token_latent_frame.reshape(sub_count, sub_rows),
    )

    def tangent_step(state, key_block):
        block_keys, block_values, block_key_dots, block_value_dots, block_frames = key_block
        allowed = allowed_for(frame_reach, block_frames)
        combined, plain_sum, curve = state
        weights = probs_of(allowed, block_keys)
        logit_dots = (
            dots_of(tangent_queries, block_keys) + dots_of(query_heads, block_key_dots)
        ) * score_scale
        curve_terms = weights * logit_dots
        weights_low = weights.astype(jnp.bfloat16)
        combined = (
            combined
            + jnp.einsum(
                "hqk,khd->qhd",
                curve_terms.astype(jnp.bfloat16),
                block_values,
                preferred_element_type=jnp.float32,
            )
            + jnp.einsum(
                "hqk,khd->qhd", weights_low, block_value_dots, preferred_element_type=jnp.float32
            )
        )
        plain_sum = plain_sum + jnp.einsum(
            "hqk,khd->qhd", weights_low, block_values, preferred_element_type=jnp.float32
        )
        return ((combined, plain_sum, curve + curve_terms.sum(-1)), None)

    result, _ = lax.scan(tangent_step, tangent_init, sub_blocks)
    combined, plain_sum, curve = result
    penalty_grad = (
        (combined - jnp.transpose(curve)[..., None] * plain_sum)
        .reshape(tok_rows, row_width)
        .astype(jnp.bfloat16)
    )
    return (grad_x, penalty_grad)


def solution(mesh):
    return jax.shard_map(
        on_device,
        mesh=mesh,
        in_specs=(P(("seq", "head"), None), P(None, None, "head"), P("seq", "head"), P(), P()),
        out_specs=(P(("seq", "head"), None), P("seq", "head")),
        check_vma=False,
    )
```

profile of v0, /device:TPU:24, one launch (start us, length us, event | category | flops | bytes accessed | tf_op | source)
XLA Modules:
  0.0 714.1 jit_solution(417699822833937658)
XLA Ops:
  7.9 29.0 %all-gather.10.cloned.1.call-done = bf16[128,5120]{1,0:T(8,128)(2,1)} async-done(((bf16[32,5120]{1,0:T(8,128)(2,1)}), bf16[128,5120]{1,0:T(8,128)(2,1)}) %all-gather.10.cloned.1.call-update) | async-done | bytes 1310736 | tf_op jit(solution)/shard_map/all_gather | solution.py:34
  36.9 12.2 %fusion.92 = bf16[3,128,640]{1,2,0:T(8,128)(2,1)S(1)} fusion(bf16[3,5120,640]{2,1,0:T(8,128)(2,1)} %param.12, bf16[128,5120]{1,0:T(8,128)(2,1)} %all-gather.10.cloned.1.call-done), kind=kOutput, calls=%fused_computation.115 | convolution fusion | flops 2516828160 | bytes 21463040 | tf_op jit(solution)/shard_map/td,cde->cte/dot_general | solution.py:35
  52.2 49.7 %all-gather.14.cloned.1.call-done = bf16[1,4096,640]{1,2,0:T(8,128)(2,1)} async-done(((bf16[1,128,640]{1,2,0:T(8,128)(2,1)}), bf16[1,4096,640]{1,2,0:T(8,128)(2,1)}) %all-gather.14.cloned.1.call-update) | async-done | bytes 5242896 | tf_op jit(solution)/shard_map/all_gather | solution.py:43
  101.9 8.3 %copy.74 = bf16[80,8,8,512]{3,2,1,0:T(8,128)(2,1)} copy(bf16[80,8,8,512]{3,1,2,0:T(8,128)(2,1)} %bitcast.272) | data formatting | bytes 10485760
  110.2 8.7 %copy.38 = bf16[8,512,5,128]{3,1,2,0:T(8,128)(2,1)} copy(bf16[8,512,5,128]{1,0,3,2:T(8,128)(2,1)} %bitcast.265) | data formatting | bytes 10485760
  118.8 37.1 %all-gather.12.cloned.1.call-done = bf16[1,4096,640]{1,2,0:T(8,128)(2,1)} async-done(((bf16[1,128,640]{1,2,0:T(8,128)(2,1)}), bf16[1,4096,640]{1,2,0:T(8,128)(2,1)}) %all-gather.12.cloned.1.call-update) | async-done | bytes 5242896 | tf_op jit(solution)/shard_map/all_gather | solution.py:42
  155.9 8.3 %copy.73 = bf16[80,8,8,512]{3,2,1,0:T(8,128)(2,1)} copy(bf16[80,8,8,512]{3,1,2,0:T(8,128)(2,1)} %bitcast.273) | data formatting | bytes 10485760
  164.3 8.6 %copy.40 = bf16[8,512,5,128]{3,1,2,0:T(8,128)(2,1)} copy(bf16[8,512,5,128]{1,0,3,2:T(8,128)(2,1)} %bitcast.271) | data formatting | bytes 10485760
  172.8 28.6 %while.45 = (s32[]{:T(128)}, f32[5,128]{1,0:T(8,128)S(1)}, f32[5,128]{1,0:T(8,128)S(1)}, f32[5,128]{1,0:T(8,128)S(1)}, s32[8,512]{1,0:T(8,128)S(1)}, /*index=5*/...) while((s32[]{:T(128)}, f32[5,128]{1,0:T(8,128)S(1)}, ...), condition=%wide.region_4.5_spmd.clone, body=%wide.region_0.4_spmd.clone.sunk | while | flops 172171648 | bytes 5888132 | solution.py:85
  201.4 57.9 %while.46 = (s32[]{:T(128)}, f32[128,5,128]{0,2,1:T(8,128)S(1)}, bf16[8,512,5,128]{3,1,2,0:T(8,128)(2,1)}, bf16[8,512,5,128]{3,1,2,0:T(8,128)(2,1)}, bf16[8,512,...) while((s32[]{:T(128)}, f32[128,5,128]{0,2,1:T(8,128)S(1)}, ...), condition=%wide.region_6.7_spmd.clone, body=%wide.region_5.6_spmd.clone.sunk | while | flops 423743488 | bytes 11943571 | solution.py:116
  259.3 6.3 copy.65
  279.5 74.0 %reduce-scatter.3.cloned.1.call-done = bf16[128,640]{1,0:T(8,128)(2,1)} async-done(((bf16[4096,640]{1,0:T(8,128)(2,1)}), bf16[128,640]{1,0:T(8,128)(2,1)}) %reduce-scatter.3.cloned.1.call-update) | async-done | bytes 163856 | tf_op jit(solution)/shard_map/reduce_scatter | solution.py:118
  353.4 87.9 %reduce-scatter.5.cloned.1.call-done = bf16[128,640]{1,0:T(8,128)(2,1)} async-done(((bf16[4096,640]{1,0:T(8,128)(2,1)}), bf16[128,640]{1,0:T(8,128)(2,1)}) %reduce-scatter.5.cloned.1.call-update) | async-done | bytes 163856 | tf_op jit(solution)/shard_map/reduce_scatter | solution.py:124
  441.4 11.4 %fusion.81 = bf16[128,5120]{1,0:T(8,128)(2,1)} fusion(bf16[3,5120,640]{2,1,0:T(8,128)(2,1)} %param.12, bf16[1,128,640]{2,1,0:T(8,128)(2,1)} %bitcast.280, bf16[1,128,640]{2,1,0:T(8,128)(2,1)} %bitcast.279, bf16[1,128,640]{2,1,0:T(8,128)(2,1)S(1)} %copy.48), kind=kOutput, calls=%fused_computation.106 | convolution fusion | flops 2517729280 | bytes 21463040 | tf_op jit(solution)/shard_map/cte,cde->td/dot_general | solution.py:134
  452.9 47.9 %all-reduce.2.cloned.1.call-done = bf16[128,5120]{1,0:T(8,128)(2,1)} async-done(((bf16[128,5120]{1,0:T(8,128)(2,1)}), bf16[128,5120]{1,0:T(8,128)(2,1)}) %all-reduce.2.cloned.1.call-update) | async-done | bytes 1310736 | tf_op jit(solution)/shard_map/psum | solution.py:135
  500.8 9.9 %fusion.95 = bf16[3,128,640]{2,1,0:T(8,128)(2,1)S(1)} fusion(bf16[3,5120,640]{2,1,0:T(8,128)(2,1)} %param.12, bf16[128,5120]{1,0:T(8,128)(2,1)} %all-reduce.2.cloned.1.call-done), kind=kOutput, calls=%fused_computation.116 | convolution fusion | flops 2516828160 | bytes 21463040 | tf_op jit(solution)/shard_map/td,cde->cte/dot_general | solution.py:138
  512.3 6.7 copy.52
  521.0 38.0 %all-gather.16.cloned.1.call-done = bf16[1,4096,640]{2,1,0:T(8,128)(2,1)} async-done(((bf16[1,128,640]{2,1,0:T(8,128)(2,1)}), bf16[1,4096,640]{2,1,0:T(8,128)(2,1)}) %all-gather.16.cloned.1.call-update) | async-done | bytes 5242896 | tf_op jit(solution)/shard_map/all_gather | solution.py:143
  559.1 12.9 %reshape.68 = bf16[8,512,5,128]{3,2,1,0:T(8,128)(2,1)} reshape(bf16[1,4096,640]{2,1,0:T(8,128)(2,1)} %all-gather.16.cloned.1.call-done) | data formatting | bytes 10485760 | tf_op jit(solution)/shard_map/reshape | solution.py:150
  571.9 7.2 %copy.56 = bf16[8,512,5,128]{3,1,2,0:T(8,128)(2,1)} copy(bf16[8,512,5,128]{3,2,1,0:T(8,128)(2,1)} %reshape.68) | data formatting | bytes 10485760
  579.2 29.5 %all-gather.18.cloned.1.call-done = bf16[1,4096,640]{2,1,0:T(8,128)(2,1)} async-done(((bf16[1,128,640]{2,1,0:T(8,128)(2,1)}), bf16[1,4096,640]{2,1,0:T(8,128)(2,1)}) %all-gather.18.cloned.1.call-update) | async-done | bytes 5242896 | tf_op jit(solution)/shard_map/all_gather | solution.py:144
  608.6 12.6 %reshape.69 = bf16[8,512,5,128]{3,2,1,0:T(8,128)(2,1)} reshape(bf16[1,4096,640]{2,1,0:T(8,128)(2,1)} %all-gather.18.cloned.1.call-done) | data formatting | bytes 10485760 | tf_op jit(solution)/shard_map/reshape | solution.py:150
  621.2 11.2 %copy.57 = bf16[8,512,5,128]{1,3,2,0:T(8,128)(2,1)} copy(bf16[8,512,5,128]{3,2,1,0:T(8,128)(2,1)} %reshape.69) | data formatting | bytes 10485760
  632.4 73.8 %while.47 = (s32[]{:T(128)}, f32[128,5,128]{0,2,1:T(8,128)S(1)}, f32[128,5,128]{0,2,1:T(8,128)S(1)}, f32[5,128]{1,0:T(8,128)S(1)}, bf16[8,512,5,128]{1,3,2,0:T(8...) while((s32[]{:T(128)}, f32[128,5,128]{0,2,1:T(8,128)S(1)}, ...), condition=%wide.region_12.13_spmd.clone, body=%wide.region_10.12_spmd.clone.sunk | while | flops 508449408 | bytes 15720093 | solution.py:187
  (242 shorter events, 180.5 us)
Async XLA Ops:
  7.2 29.8 %all-gather.10.cloned.1.call-start = ((), (), s32[]{:S(2)}) async-start(), calls=%async_computation.2 | async-start | bytes 1638400 | tf_op jit(solution)/shard_map/all_gather | solution.py:34
  7.9 94.0 %all-gather.14.cloned.1.call-start = ((), (), s32[]{:S(2)}) async-start(), calls=%async_computation.7 | async-start | bytes 5406720 | tf_op jit(solution)/shard_map/all_gather | solution.py:43
  49.2 2.2 copy-start.1
  49.2 2.3 copy-start
  49.2 2.6 copy-start.2
  50.0 105.9 %all-gather.12.cloned.1.call-start = ((), (), s32[]{:S(2)}) async-start(), calls=%async_computation.6 | async-start | bytes 5406720 | tf_op jit(solution)/shard_map/all_gather | solution.py:42
  50.7 302.7 %reduce-scatter.3.cloned.1.call-start = ((), (), s32[]{:S(2)}) async-start(), calls=%async_computation.3 | async-start | bytes 5406720 | tf_op jit(solution)/shard_map/reduce_scatter | solution.py:118
  269.2 172.2 %reduce-scatter.5.cloned.1.call-start = ((), (), s32[]{:S(2)}) async-start(), calls=%async_computation.4 | async-start | bytes 5406720 | tf_op jit(solution)/shard_map/reduce_scatter | solution.py:124
  279.2 221.6 %all-reduce.2.cloned.1.call-start = ((), (), s32[]{:S(2)}) async-start(), calls=%async_computation.5 | async-start | bytes 2621440 | tf_op jit(solution)/shard_map/psum | solution.py:135
  452.8 106.2 %all-gather.16.cloned.1.call-start = ((), (), s32[]{:S(2)}) async-start(), calls=%async_computation.8 | async-start | bytes 5406720 | tf_op jit(solution)/shard_map/all_gather | solution.py:143
  511.5 97.1 %all-gather.18.cloned.1.call-start = ((), (), s32[]{:S(2)}) async-start(), calls=%async_computation.9 | async-start | bytes 5406720 | tf_op jit(solution)/shard_map/all_gather | solution.py:144
Sparse Core Ops, SparseCore 0:
  9.7 27.2 all-gather.9
  50.1 51.7 all-gather.13
  104.6 51.2 all-gather.11
  269.3 84.0 reduce-scatter.2
  357.5 83.8 reduce-scatter.4
  453.0 47.8 all-reduce.1
  511.6 47.3 all-gather.15
  561.9 46.6 all-gather.17
where the time goes:
time: 726 us; the launch traced here: 714 us
  waiting for transfers between devices  395 us (54%)
  matrix products  190 us (26%)
  local copies, waits for them, and re-layouts  110 us (15%)
  between operations  14.6 us (2%)
    reduce_scatter x1, waiting for transfers between devices, on_device(): lax.psum_scatter(value_parts.reshape(all_tokens, row_width).astype(jnp.bf...  87.9 us
    dot_general x56, matrix products, dots_of(): jnp.einsum('qhd,khd->hqk', left_side, right_side, preferred_element_type=...  84.2 us
    reduce_scatter x1, waiting for transfers between devices, on_device(): lax.psum_scatter(key_parts.reshape(all_tokens, row_width).astype(jnp.bflo...  74 us
    unnamed x20, local copies, waits for them, and re-layouts  67.7 us
    all_gather x1, waiting for transfers between devices, on_device(): lax.all_gather(values_own, 'seq', axis=0, tiled=True)  49.7 us
    psum x1, waiting for transfers between devices, on_device(): input_sum = lax.psum(partial_input.astype(jnp.bfloat16), 'head')  47.9 us
    all_gather x1, waiting for transfers between devices, on_device(): key_tangent = lax.all_gather(tangents[1], 'seq', axis=0, tiled=True)  38 us
    all_gather x1, waiting for transfers between devices, on_device(): lax.all_gather(keys_own, 'seq', axis=0, tiled=True)  37.1 us
  transfers between devices with their start and end apart: 8, of which 8 were waited for; matrix products, arithmetic and copies ran while one was open for 8% of the time, Pallas kernels for 0%

commit v1 on v0

v1 whole, which is shorter than its diff:
```python
import functools
import math

import jax
import jax.numpy as jnp
from jax import lax
from jax.experimental import pallas as pl
from jax.experimental.pallas import tpu as pltpu
from jax.sharding import PartitionSpec as P

HD = 128
MESH = pl.DeviceIdType.MESH
LOG2E = math.log2(math.e)
BARRED = -1e30

CHIPS = 16
BUSY = 15
HEADS = 5
SLOTS = 6


def start_of(third):
    return (CHIPS * third + 2) // 3


def third_of(chip):
    return (chip * 3) // CHIPS


def place():
    me = lax.axis_index("seq")
    return me // 2, me % 2


def enter(chip, core):
    barrier = pltpu.get_barrier_semaphore()

    def greet(step, carry):
        peer = (chip + step) % CHIPS
        pl.semaphore_signal(barrier, inc=1, device_id={"seq": 2 * peer + core}, device_id_type=MESH)
        return carry

    lax.fori_loop(1, CHIPS, greet, 0)
    pl.semaphore_signal(barrier, inc=1, device_id={"seq": 2 * chip + 1 - core}, device_id_type=MESH)
    pl.semaphore_wait(barrier, CHIPS)


def remote(src, dst, send_sem, recv_sem, device):
    return pltpu.make_async_remote_copy(
        src_ref=src,
        dst_ref=dst,
        send_sem=send_sem,
        recv_sem=recv_sem,
        device_id={"seq": device},
        device_id_type=MESH,
    )


def deal_kernel(kv_ref, q_ref, kv_out, q_out, kv_send, kv_recv, pass_send, pass_recv, q_send, q_recv):
    chip, core = place()
    partner = 2 * chip + 1 - core
    third = third_of(chip)
    slot = chip - start_of(third)
    enter(chip, core)

    def kv_copy(d):
        return remote(
            kv_ref.at[:, d // 3], kv_out.at[:, chip, core], kv_send.at[d], kv_recv.at[chip], 2 * d + core
        )

    def q_copy(h):
        return remote(q_ref.at[:, h], q_out.at[:, slot], q_send.at[h], q_recv.at[slot], 2 * (3 * h + third) + core)

    def own_kv():
        return pltpu.make_async_copy(kv_ref.at[:, chip // 3], kv_out.at[:, chip, core], kv_recv.at[chip])

    def own_q():
        return pltpu.make_async_copy(q_ref.at[:, chip // 3], q_out.at[:, slot], q_recv.at[slot])

    def send_q(h, carry):
        @pl.when(3 * h + third != chip)
        def _():
            q_copy(h).start()

        @pl.when(3 * h + third == chip)
        def _():
            own_q().start()

        return carry

    def send_kv(step, carry):
        d = (chip + step) % CHIPS

        @pl.when(jnp.logical_and(d < BUSY, step > 0))
        def _():
            kv_copy(d).start()

        @pl.when(jnp.logical_and(d < BUSY, step == 0))
        def _():
            own_kv().start()

        return carry

    lax.fori_loop(0, CHIPS, send_kv, 0)
    lax.fori_loop(0, HEADS, send_q, 0)

    own_third = chip % 3
    first = start_of(own_third)
    count = start_of(own_third + 1) - first

    def pass_copy(source):
        return remote(
            kv_out.at[:, source, core],
            kv_out.at[:, source, core],
            pass_send.at[source],
            pass_recv.at[source],
            partner,
        )

    def pass_wait(source):
        return remote(
            kv_out.at[:, source, 1 - core],
            kv_out.at[:, source, 1 - core],
            pass_send.at[source],
            pass_recv.at[source],
            partner,
        )

    @pl.when(chip < BUSY)
    def _():
        def arrive(step, carry):
            source = (chip + CHIPS - step) % CHIPS

            @pl.when(step > 0)
            def _():
                remote(
                    kv_ref.at[:, 0], kv_out.at[:, source, core], kv_send.at[0], kv_recv.at[source], partner
                ).wait_recv()

            @pl.when(step == 0)
            def _():
                own_kv().wait()

            pass_copy(source).start()
            return carry

        lax.fori_loop(0, CHIPS, arrive, 0)

        def arrive_q(n, carry):
            @pl.when(first + n != chip)
            def _():
                remote(q_ref.at[:, 0], q_out.at[:, n], q_send.at[0], q_recv.at[n], partner).wait_recv()

            @pl.when(first + n == chip)
            def _():
                own_q().wait()

            return carry

        lax.fori_loop(0, count, arrive_q, 0)

        @pl.when(count < SLOTS)
        def _():
            q_out[:, SLOTS - 1] = jnp.zeros_like(q_out[:, SLOTS - 1])

        def passed(step, carry):
            source = (chip + CHIPS - step) % CHIPS
            pass_wait(source).wait_recv()
            pass_copy(source).wait_send()
            return carry

        lax.fori_loop(0, CHIPS, passed, 0)

    def sent_kv(step, carry):
        d = (chip + step) % CHIPS

        @pl.when(d < BUSY)
        def _():
            kv_copy(d).wait_send()

        return carry

    lax.fori_loop(1, CHIPS, sent_kv, 0)

    def sent_q(h, carry):
        @pl.when(3 * h + third != chip)
        def _():
            q_copy(h).wait_send()

        return carry

    lax.fori_loop(0, HEADS, sent_q, 0)


VMEM = pl.BlockSpec(memory_space=pltpu.VMEM)
DMA = pltpu.SemaphoreType.DMA


def deal(kv, q, collective_id):
    parts = q.shape[0]
    return pl.pallas_call(
        deal_kernel,
        out_shape=(
            jax.ShapeDtypeStruct((2, CHIPS, 2, HD, HD), jnp.bfloat16),
            jax.ShapeDtypeStruct((parts, SLOTS, HD, HD), jnp.bfloat16),
        ),
        in_specs=[VMEM] * 2,
        out_specs=(VMEM, VMEM),
        scratch_shapes=[
            DMA((CHIPS,)),
            DMA((CHIPS,)),
            DMA((CHIPS,)),
            DMA((CHIPS,)),
            DMA((HEADS,)),
            DMA((SLOTS,)),
        ],
        compiler_params=pltpu.CompilerParams(
            collective_id=collective_id, has_side_effects=True, vmem_limit_bytes=32 << 20
        ),
        name="deal",
    )(kv, q)


def give_back(chip, core, src, dst, send, recv):
    own_third = chip % 3
    first = start_of(own_third)
    count = start_of(own_third + 1) - first
    third = third_of(chip)
    own_head = chip // 3

    def out_copy(n):
        return remote(src.at[n], dst.at[own_head], send.at[n], recv.at[own_head], 2 * (first + n) + core)

    def own():
        return pltpu.make_async_copy(src.at[chip - first], dst.at[own_head], recv.at[own_head])

    def begin():
        @pl.when(chip < BUSY)
        def _():
            def go(n, carry):
                @pl.when(first + n != chip)
                def _():
                    out_copy(n).start()

                @pl.when(first + n == chip)
                def _():
                    own().start()

                return carry

            lax.fori_loop(0, count, go, 0)

    def end():
        def come(h, carry):
            @pl.when(3 * h + third != chip)
            def _():
                remote(src.at[0], dst.at[h], send.at[0], recv.at[h], 2 * chip + 1 - core).wait_recv()

            @pl.when(3 * h + third == chip)
            def _():
                own().wait()

            return carry

        lax.fori_loop(0, HEADS, come, 0)

        @pl.when(chip < BUSY)
        def _():
            def gone(n, carry):
                @pl.when(first + n != chip)
                def _():
                    out_copy(n).wait_send()

                return carry

            lax.fori_loop(0, count, gone, 0)

    return begin, end


def return_kernel(dq_ref, q_out, q_send, q_recv):
    chip, core = place()
    enter(chip, core)
    begin, end = give_back(chip, core, dq_ref, q_out, q_send, q_recv)
    begin()
    end()


def return_queries(dq, collective_id):
    return pl.pallas_call(
        return_kernel,
        out_shape=jax.ShapeDtypeStruct((HEADS, HD, HD), jnp.bfloat16),
        in_specs=[VMEM],
        out_specs=VMEM,
        scratch_shapes=[DMA((SLOTS,)), DMA((HEADS,))],
        compiler_params=pltpu.CompilerParams(
            collective_id=collective_id, has_side_effects=True, vmem_limit_bytes=32 << 20
        ),
        name="return_queries",
    )(dq)


def reduce_kernel(
    dkv_ref, dq_ref, kv_sum, q_out, other, mixed, landed, x_send, x_recv, kv_send, kv_recv, q_send, q_recv
):
    chip, core = place()
    partner = 2 * chip + 1 - core
    enter(chip, core)
    begin, end = give_back(chip, core, dq_ref, q_out, q_send, q_recv)

    def swap(target):
        return remote(
            dkv_ref.at[:, target, 1 - core], other.at[:, target], x_send.at[target], x_recv.at[target], partner
        )

    def out_copy(target):
        return remote(
            mixed.at[:, target], landed.at[chip], kv_send.at[target], kv_recv.at[chip], 2 * target + core
        )

    def own():
        return pltpu.make_async_copy(mixed.at[:, chip], landed.at[chip], kv_recv.at[chip])

    @pl.when(chip < BUSY)
    def _():
        def start_swap(step, carry):
            swap((chip + step) % CHIPS).start()
            return carry

        lax.fori_loop(0, CHIPS, start_swap, 0)

    begin()

    @pl.when(chip < BUSY)
    def _():
        def mix(step, carry):
            target = (chip + step) % CHIPS
            swap(target).wait_recv()
            mixed[:, target] = (
                dkv_ref[:, target, core].astype(jnp.float32) + other[:, target].astype(jnp.float32)
            ).astype(jnp.bfloat16)

            @pl.when(step > 0)
            def _():
                out_copy(target).start()

            @pl.when(step == 0)
            def _():
                own().start()

            return carry

        lax.fori_loop(0, CHIPS, mix, 0)

    def come(step, carry):
        source = (chip + CHIPS - step) % CHIPS

        @pl.when(jnp.logical_and(source < BUSY, step > 0))
        def _():
            remote(
                mixed.at[:, 0], landed.at[source], kv_send.at[0], kv_recv.at[source], partner
            ).wait_recv()

        @pl.when(jnp.logical_and(source < BUSY, step == 0))
        def _():
            own().wait()

        return carry

    lax.fori_loop(0, CHIPS, come, 0)

    def add_up(h, carry):
        total = landed[3 * h].astype(jnp.float32) + landed[3 * h + 1].astype(jnp.float32)
        kv_sum[:, h] = (total + landed[3 * h + 2].astype(jnp.float32)).astype(jnp.bfloat16)
        return carry

    lax.fori_loop(0, HEADS, add_up, 0)
    end()

    @pl.when(chip < BUSY)
    def _():
        def gone(step, carry):
            target = (chip + step) % CHIPS
            swap(target).wait_send()

            @pl.when(step > 0)
            def _():
                out_copy(target).wait_send()

            return carry

        lax.fori_loop(0, CHIPS, gone, 0)


def reduce_back(dkv, dq, collective_id):
    return pl.pallas_call(
        reduce_kernel,
        out_shape=(
            jax.ShapeDtypeStruct((2, HEADS, HD, HD), jnp.bfloat16),
            jax.ShapeDtypeStruct((HEADS, HD, HD), jnp.bfloat16),
        ),
        in_specs=[VMEM] * 2,
        out_specs=(VMEM, VMEM),
        scratch_shapes=[
            pltpu.VMEM((2, CHIPS, HD, HD), jnp.bfloat16),
            pltpu.VMEM((2, CHIPS, HD, HD), jnp.bfloat16),
            pltpu.VMEM((CHIPS, 2, HD, HD), jnp.bfloat16),
            DMA((CHIPS,)),
            DMA((CHIPS,)),
            DMA((CHIPS,)),
            DMA((CHIPS,)),
            DMA((SLOTS,)),
            DMA((HEADS,)),
        ],
        compiler_params=pltpu.CompilerParams(
            collective_id=collective_id, has_side_effects=True, vmem_limit_bytes=32 << 20
        ),
        name="reduce_back",
    )(dkv, dq)


TOKENS = 4096
ROWS = SLOTS * HD
CHUNK = 256
SCALE = HD ** (-0.5)


def nt(left, right):
    return lax.dot_general(left, right, (((1,), (1,)), ((), ())), preferred_element_type=jnp.float32)


def nn(left, right):
    return lax.dot_general(left, right, (((1,), (0,)), ((), ())), preferred_element_type=jnp.float32)


def tn(left, right):
    return lax.dot_general(left, right, (((0,), (0,)), ((), ())), preferred_element_type=jnp.float32)


def rows_of(chunk):
    return pl.ds(pl.multiple_of(chunk * CHUNK, CHUNK), CHUNK)


def grads_kernel(kv_ref, qr_ref, key_hot, row_bar, dkv_ref, dq_ref, norm_ref, k_wide, q_wide, dq_acc):
    k_wide[:, :HD] = kv_ref[0]
    k_wide[:, HD:] = key_hot[...]
    q_wide[:, :HD] = qr_ref[0]
    q_wide[:, HD:] = row_bar[...]
    factor = SCALE * LOG2E

    def stats(chunk, carry):
        top, total, weighted = carry
        rows = rows_of(chunk)
        raw = nt(k_wide[rows, :], q_wide[...])
        dots = nt(kv_ref[1, rows, :], qr_ref[1])
        new_top = jnp.maximum(top, raw.max(axis=0, keepdims=True))
        weights = jnp.exp2((raw - new_top) * factor)
        shrink = jnp.exp2((top - new_top) * factor)
        return (
            new_top,
            total * shrink + weights.sum(axis=0, keepdims=True),
            weighted * shrink + (weights * dots).sum(axis=0, keepdims=True),
        )

    zero = jnp.zeros((1, ROWS), jnp.float32)
    top, total, weighted = lax.fori_loop(
        0, TOKENS // CHUNK, stats, (jnp.full((1, ROWS), BARRED, jnp.float32), zero, zero)
    )
    norm = top * factor + jnp.log2(total)
    row_dots = weighted / total
    norm_ref[...] = norm
    dq_acc[...] = jnp.zeros_like(dq_acc)

    def grads(chunk, carry):
        rows = rows_of(chunk)
        raw = nt(k_wide[rows, :], q_wide[...])
        dots = nt(kv_ref[1, rows, :], qr_ref[1])
        weights = jnp.exp2(raw * factor - norm)
        slopes = (weights * (dots - row_dots)).astype(jnp.bfloat16)
        dkv_ref[0, rows, :] = (SCALE * nn(slopes, qr_ref[0])).astype(jnp.bfloat16)
        dkv_ref[1, rows, :] = nn(weights.astype(jnp.bfloat16), qr_ref[1]).astype(jnp.bfloat16)
        dq_acc[...] += tn(kv_ref[0, rows, :], slopes)
        return carry

    lax.fori_loop(0, TOKENS // CHUNK, grads, 0)
    dq_ref[...] = (SCALE * dq_acc[...]).T.astype(jnp.bfloat16)


def attention_grads(kv, qr, key_hot, row_bar):
    return pl.pallas_call(
        grads_kernel,
        out_shape=(
            jax.ShapeDtypeStruct((2, TOKENS, HD), jnp.bfloat16),
            jax.ShapeDtypeStruct((ROWS, HD), jnp.bfloat16),
            jax.ShapeDtypeStruct((1, ROWS), jnp.float32),
        ),
        in_specs=[VMEM] * 4,
        out_specs=(VMEM, VMEM, VMEM),
        scratch_shapes=[
            pltpu.VMEM((TOKENS, 2 * HD), jnp.bfloat16),
            pltpu.VMEM((ROWS, 2 * HD), jnp.bfloat16),
            pltpu.VMEM((HD, ROWS), jnp.float32),
        ],
        compiler_params=pltpu.CompilerParams(vmem_limit_bytes=48 << 20),
        name="attention_grads",
    )(kv, qr, key_hot, row_bar)


def tangent_kernel(
    kv_ref, q_ref, dot_ref, qdot_ref, key_hot, row_bar, norm_ref, out_ref, k_wide, q_wide, kk_wide, qq_wide, vv_wide, acc, plain
):
    k_wide[:, :HD] = kv_ref[0]
    k_wide[:, HD:] = key_hot[...]
    q_wide[:, :HD] = q_ref[...]
    q_wide[:, HD:] = row_bar[...]
    kk_wide[:, :HD] = kv_ref[0]
    kk_wide[:, HD:] = dot_ref[0]
    qq_wide[:, :HD] = qdot_ref[...]
    qq_wide[:, HD:] = q_ref[...]
    vv_wide[:, :HD] = kv_ref[1]
    vv_wide[:, HD:] = dot_ref[1]
    factor = SCALE * LOG2E
    norm = norm_ref[...]
    acc[...] = jnp.zeros_like(acc)
    plain[...] = jnp.zeros_like(plain)

    def step(chunk, curve):
        rows = rows_of(chunk)
        raw = nt(k_wide[rows, :], q_wide[...])
        moved = nt(kk_wide[rows, :], qq_wide[...])
        weights = jnp.exp2(raw * factor - norm)
        turned = weights * (moved * SCALE)
        acc[...] += tn(kv_ref[1, rows, :], turned.astype(jnp.bfloat16))
        plain[...] += tn(vv_wide[rows, :], weights.astype(jnp.bfloat16))
        return curve + turned.sum(axis=0, keepdims=True)

    curve = lax.fori_loop(0, TOKENS // CHUNK, step, jnp.zeros((1, ROWS), jnp.float32))
    total = acc[...] + plain[HD:, :] - curve * plain[:HD, :]
    out_ref[...] = total.T.astype(jnp.bfloat16)


def attention_tangent(kv, q, dots, qdot, key_hot, row_bar, norm):
    return pl.pallas_call(
        tangent_kernel,
        out_shape=jax.ShapeDtypeStruct((ROWS, HD), jnp.bfloat16),
        in_specs=[VMEM] * 7,
        out_specs=VMEM,
        scratch_shapes=[
            pltpu.VMEM((TOKENS, 2 * HD), jnp.bfloat16),
            pltpu.VMEM((ROWS, 2 * HD), jnp.bfloat16),
            pltpu.VMEM((TOKENS, 2 * HD), jnp.bfloat16),
            pltpu.VMEM((ROWS, 2 * HD), jnp.bfloat16),
            pltpu.VMEM((TOKENS, 2 * HD), jnp.bfloat16),
            pltpu.VMEM((HD, ROWS), jnp.float32),
            pltpu.VMEM((2 * HD, ROWS), jnp.float32),
        ],
        compiler_params=pltpu.CompilerParams(vmem_limit_bytes=48 << 20),
        name="attention_tangent",
    )(kv, q, dots, qdot, key_hot, row_bar, norm)


def mask_sides(token_latent_frame, frame_mask):
    frame_count = frame_mask.shape[0]
    lanes = jnp.arange(HD, dtype=jnp.int32)
    key_hot = (token_latent_frame[:, None] == lanes).astype(jnp.bfloat16)
    chip, core = place()
    first = start_of(chip % 3)
    blocks = token_latent_frame.reshape(CHIPS, 2, HD)
    mine = jnp.minimum(first + jnp.arange(SLOTS, dtype=jnp.int32), CHIPS - 1)
    own_frames = blocks[mine, core].reshape(ROWS)
    barred = jnp.pad(jnp.where(frame_mask == 1, 0.0, 1.0), ((0, 0), (0, HD - frame_count)))
    own_hot = (own_frames[:, None] == jnp.arange(frame_count, dtype=jnp.int32)).astype(jnp.float32)
    row_bar = (jnp.dot(own_hot, barred) * BARRED).astype(jnp.bfloat16)
    return key_hot, row_bar


def by_head(rows):
    return jnp.swapaxes(rows.reshape(rows.shape[:-1] + (HEADS, HD)), -3, -2)


def to_rows(heads):
    swapped = jnp.swapaxes(heads, -3, -2)
    return swapped.reshape(swapped.shape[:-2] + (HEADS * HD,))


def on_device(clip_tokens, w_qkv, readout, token_latent_frame, frame_mask):
    key_hot, row_bar = mask_sides(token_latent_frame, frame_mask)
    tokens_all = lax.all_gather(clip_tokens, "head", axis=0, tiled=True)
    projected = jnp.einsum(
        "td,cde->cte", tokens_all, w_qkv, preferred_element_type=jnp.float32
    ).astype(jnp.bfloat16)
    heads = by_head(projected)
    kv, qr = deal(heads[1:], jnp.stack([heads[0], by_head(readout)]), 0)
    kv = kv.reshape(2, TOKENS, HD)
    qr = qr.reshape(2, ROWS, HD)
    dkv, dq, norm = attention_grads(kv, qr, key_hot, row_bar)
    kv_grad, q_grad = reduce_back(
        dkv.reshape(2, CHIPS, 2, HD, HD), dq.reshape(SLOTS, HD, HD), 1
    )
    grads = to_rows(jnp.concatenate([q_grad[None], kv_grad]))
    partial_input = jnp.einsum("cte,cde->td", grads, w_qkv, preferred_element_type=jnp.float32)
    input_sum = lax.psum(partial_input.astype(jnp.bfloat16), "head")
    panel_rows = clip_tokens.shape[0]
    grad_x = lax.dynamic_slice_in_dim(input_sum, lax.axis_index("head") * panel_rows, panel_rows)
    tangents = jnp.einsum(
        "td,cde->cte", input_sum, w_qkv, preferred_element_type=jnp.float32
    ).astype(jnp.bfloat16)
    dot_heads = by_head(tangents)
    kv_dot, q_dot = deal(dot_heads[1:], dot_heads[:1], 2)
    out = attention_tangent(
        kv, qr[0], kv_dot.reshape(2, TOKENS, HD), q_dot.reshape(ROWS, HD), key_hot, row_bar, norm
    )
    penalty_grad = to_rows(return_queries(out.reshape(SLOTS, HD, HD), 3))
    return (grad_x, penalty_grad)


def solution(mesh):
    return jax.shard_map(
        on_device,
        mesh=mesh,
        in_specs=(P(("seq", "head"), None), P(None, None, "head"), P("seq", "head"), P(), P()),
        out_specs=(P(("seq", "head"), None), P("seq", "head")),
        check_vma=False,
    )
```

time: 726 us -> 254 us (0.35); the launches traced: 714 us -> 254 us
  waiting for transfers between devices: 395 us -> 71.2 us
  matrix products: 190 us -> 35.3 us
  Pallas kernels: 0 us -> 114 us
  local copies, waits for them, and re-layouts: 110 us -> 15.3 us
    reduce_scatter x2 -> x0, waiting for transfers between devices: 162 us -> none  [the longest x1 87.9 us: on_device(): lax.psum_scatter(value_parts.reshape(all_tokens, row_width).astype(jnp.bf...]
    dot_general x129 -> x1, matrix products: 156 us -> 0.97 us  [mask_sides(): row_bar = (jnp.dot(own_hot, barred) * BARRED).astype(jnp.bfloat16)]
    all_gather x4 -> x0, waiting for transfers between devices: 154 us -> none  [the longest x1 49.7 us: on_device(): lax.all_gather(values_own, 'seq', axis=0, tiled=True)]
    pallas_call x0 -> x6, Pallas kernels: none -> 114 us  [the longest x2 48.5 us: deal(): pl.pallas_call(deal_kernel, out_shape=(jax.ShapeDtypeStruct((2, CHIPS, 2,...]
    unnamed x20 -> x8, local copies, waits for them, and re-layouts: 67.7 us -> 2.82 us
    reshape x3, local copies, waits for them, and re-layouts: 25.5 us -> 2.49 us  [by_head(): return jnp.swapaxes(rows.reshape(rows.shape[:-1] + (HEADS, HD)), -3, -2)]
    convert_element_type x2 -> x1, local copies, waits for them, and re-layouts: 12.5 us -> 2.07 us  [on_device(): tangents = jnp.einsum('td,cde->cte', input_sum, w_qkv, preferred_element_...]
  transfers between devices with their start and end apart: 8 -> 2, of which waited for: 8 -> 2; matrix products, arithmetic and copies ran while one was open for 8% -> 3% of each run, Pallas kernels for 0% -> 0%
where the time goes in v1:
time: 254 us
  Pallas kernels  114 us (45%)
  waiting for transfers between devices  71.2 us (28%)
  matrix products  35.3 us (14%)
  local copies, waits for them, and re-layouts  15.3 us (6%)
  between operations  14.2 us (6%)
  other arithmetic  4.04 us (2%)
    pallas_call x2, Pallas kernels, deal(): pl.pallas_call(deal_kernel, out_shape=(jax.ShapeDtypeStruct((2, CHIPS, 2,...  48.5 us
    psum x1, waiting for transfers between devices, on_device(): input_sum = lax.psum(partial_input.astype(jnp.bfloat16), 'head')  48.3 us
    pallas_call x1, Pallas kernels, reduce_back(): pl.pallas_call(reduce_kernel, out_shape=(jax.ShapeDtypeStruct((2, HEADS,...  23.3 us
    all_gather x1, waiting for transfers between devices, on_device(): tokens_all = lax.all_gather(clip_tokens, 'head', axis=0, tiled=True)  22.2 us
    pallas_call x1, Pallas kernels, attention_grads(): pl.pallas_call(grads_kernel, out_shape=(jax.ShapeDtypeStruct((2, TOKENS,...  19.2 us
    pallas_call x1, Pallas kernels, attention_tangent(): pl.pallas_call(tangent_kernel, out_shape=jax.ShapeDtypeStruct((ROWS, HD),...  12.7 us
    dot_general x1, matrix products, on_device(): jnp.einsum('td,cde->cte', tokens_all, w_qkv, preferred_element_type=jnp.f...  12.2 us
    dot_general x1, matrix products, on_device(): jnp.einsum('cte,cde->td', grads, w_qkv, preferred_element_type=jnp.float32)  11.4 us
  transfers between devices with their start and end apart: 2, of which 2 were waited for; matrix products, arithmetic and copies ran while one was open for 3% of the time, Pallas kernels for 0%

profile of v1, /device:TPU:24, one launch (start us, length us, event | category | flops | bytes accessed | tf_op | source)
XLA Modules:
  0.0 253.7 jit_solution(16942148168593075855)
XLA Ops:
  8.0 1.1 copy.10
  9.3 1.3 gather_fusion
  11.3 1.0 fusion.15.row_bar
  12.3 2.5 fusion.1.key_hot
  14.8 22.2 %all-gather.2.cloned.1.call-done = bf16[128,5120]{1,0:T(8,128)(2,1)} async-done(((bf16[32,5120]{1,0:T(8,128)(2,1)}), bf16[128,5120]{1,0:T(8,128)(2,1)}) %all-gather.2.cloned.1.call-update) | async-done | bytes 1310736 | tf_op jit(solution)/shard_map/all_gather | solution.py:588
  36.9 12.2 %fusion.9 = bf16[3,640,128]{2,1,0:T(8,128)(2,1)S(1)} fusion(bf16[3,5120,640]{2,1,0:T(8,128)(2,1)} %param.6, bf16[128,5120]{1,0:T(8,128)(2,1)} %all-gather.2.cloned.1.call-done), kind=kOutput, calls=%fused_computation.10 | convolution fusion | flops 2516828160 | bytes 21463040 | tf_op jit(solution)/shard_map/td,cde->cte/dot_general | solution.py:589
  49.5 25.3 %deal.2 = (bf16[2,16,2,128,128]{4,3,2,1,0:T(8,128)(2,1)S(1)}, bf16[2,6,128,128]{3,2,1,0:T(8,128)(2,1)S(1)}) custom-call(bf16[2,5,128,128]{3,2,1,0:T(8,128)(2,1)S(1)} %slice.23.kv_ref, bf16[2,5,128,128]{3,2,1,0:T(8,128)(2,1)S(1)} %pad_maximum_fusion.q_ref), custom_call_target="tpu_custom_call" | custom-call | tf_op jit(solution)/shard_map/deal/pallas_call | solution.py:201
  74.9 0.9 copy-done
  75.8 19.2 %attention_grads.1 = (bf16[2,4096,128]{2,1,0:T(8,128)(2,1)S(1)}, bf16[768,128]{1,0:T(8,128)(2,1)S(1)}, f32[1,768]{1,0:T(1,128)S(1)}) custom-call(bf16[2,4096,128]{2,1,0:T(8,128)(2,1)S(1)} %bitcast.50, bf16[2,768,128]{2,1,0:T(8,128)(2,1)S(1)} %bitcast.54, bf16[4096,128]{1,0:T(8,128)(2,1)S(1)} %fusion.1.key_hot, bf16[768,128]{1,0:T(8,128)(2,1)S(1)} %copy-done), custom_call_target="tpu_custom_call" | custom-call | tf_op jit(solution)/shard_map/attention_grads/pallas_call | solution.py:490
  95.0 23.3 %reduce_back.1 = (bf16[2,5,128,128]{3,2,1,0:T(8,128)(2,1)S(1)}, bf16[5,128,128]{2,1,0:T(8,128)(2,1)S(1)}) custom-call(bf16[2,16,2,128,128]{4,3,2,1,0:T(8,128)(2,1)S(1)} %bitcast.53, bf16[6,128,128]{2,1,0:T(8,128)(2,1)S(1)} %bitcast.59), custom_call_target="tpu_custom_call" | custom-call | tf_op jit(solution)/shard_map/reduce_back/pallas_call | solution.py:396
  118.3 0.8 maximum_bitcast_fusion
  119.1 2.0 copy.12
  121.2 11.4 %fusion = bf16[128,5120]{1,0:T(8,128)(2,1)} fusion(bf16[3,128,640]{1,2,0:T(8,128)(2,1)} %bitcast.66, bf16[3,5120,640]{2,1,0:T(8,128)(2,1)} %param.6), kind=kOutput, calls=%fused_computation.2 | convolution fusion | flops 2517237760 | bytes 21463040 | tf_op jit(solution)/shard_map/cte,cde->td/dot_general | solution.py:601
  133.2 48.3 %all-reduce.4.cloned.1.call-done = bf16[128,5120]{1,0:T(8,128)(2,1)} async-done(((bf16[128,5120]{1,0:T(8,128)(2,1)}), bf16[128,5120]{1,0:T(8,128)(2,1)}) %all-reduce.4.cloned.1.call-update) | async-done | bytes 1310736 | tf_op jit(solution)/shard_map/psum | solution.py:602
  181.5 10.7 %fusion.12 = bf16[3,128,640]{2,1,0:T(8,128)(2,1)} fusion(bf16[3,5120,640]{2,1,0:T(8,128)(2,1)} %param.6, bf16[128,5120]{1,0:T(8,128)(2,1)} %all-reduce.4.cloned.1.call-done), kind=kOutput, calls=%fused_computation.11 | convolution fusion | flops 2516828160 | bytes 21463040 | tf_op jit(solution)/shard_map/td,cde->cte/dot_general | solution.py:605
  192.2 2.1 copy.14
  194.3 2.0 copy.15
  196.3 0.9 slice.26.q_ref
  197.3 1.0 slice.25.kv_ref
  198.3 23.2 %deal.3 = (bf16[2,16,2,128,128]{4,3,2,1,0:T(8,128)(2,1)S(1)}, bf16[1,6,128,128]{3,2,1,0:T(8,128)(2,1)S(1)}) custom-call(bf16[2,5,128,128]{3,2,1,0:T(8,128)(2,1)S(1)} %slice.25.kv_ref, bf16[1,5,128,128]{3,2,1,0:T(8,128)(2,1)S(1)} %slice.26.q_ref), custom_call_target="tpu_custom_call" | custom-call | tf_op jit(solution)/shard_map/deal/pallas_call | solution.py:201
  221.5 12.7 %attention_tangent.1 = bf16[768,128]{1,0:T(8,128)(2,1)S(1)} custom-call(bf16[2,4096,128]{2,1,0:T(8,128)(2,1)S(1)} %bitcast.51, bf16[768,128]{1,0:T(8,128)(2,1)S(1)} %bitcast.55, bf16[2,4096,128]{2,1,0:T(8,128)(2,1)S(1)} %bitcast.52, bf16[768,128]{1,0:T(8,128)(2,1)S(1)} %bitcast.58, bf16[4096,128]{1,0:T(8,128)(2,1)S(1)} %fusion.1.key_hot, ...), custom_call_target="tpu_custom_call" | custom-call | tf_op jit(solution)/shard_map/attention_tangent/pallas_call | solution.py:543
  234.2 10.0 %return_queries.1 = bf16[5,128,128]{2,1,0:T(8,128)(2,1)S(1)} custom-call(bf16[6,128,128]{2,1,0:T(8,128)(2,1)S(1)} %bitcast.56), custom_call_target="tpu_custom_call" | custom-call | tf_op jit(solution)/shard_map/return_queries/pallas_call | solution.py:290
  244.3 0.8 copy.17
  245.2 1.7 constant_dynamic-slice_fusion
  (18 shorter events, 2.9 us)
Async XLA Ops:
  7.2 29.8 %all-gather.2.cloned.1.call-start = ((), (), s32[]{:S(2)}) async-start(), calls=%async_computation | async-start | bytes 1638400 | tf_op jit(solution)/shard_map/all_gather | solution.py:588
  7.9 173.6 %all-reduce.4.cloned.1.call-start = ((), (), s32[]{:S(2)}) async-start(), calls=%async_computation.1 | async-start | bytes 2621440 | tf_op jit(solution)/shard_map/psum | solution.py:602
  74.9 0.9 copy-start
  192.2 29.2 %copy-start.1 = (bf16[768,128]{1,0:T(8,128)(2,1)S(1)}, bf16[768,128]{1,0:T(8,128)(2,1)}, u32[]{:S(2)}) copy-start(bf16[768,128]{1,0:T(8,128)(2,1)} %fusion.15.row_bar) | copy-start | bytes 589828
  192.2 29.2 %copy-start.2 = (bf16[1,6,128,128]{3,2,1,0:T(8,128)(2,1)S(1)}, bf16[1,6,128,128]{3,2,1,0:T(8,128)(2,1)}, u32[]{:S(2)}) copy-start(bf16[1,6,128,128]{3,2,1,0:T(8,128)(2,1)} %slice.18) | copy-start | bytes 589828
Sparse Core Ops, SparseCore 0:
  9.7 27.2 all-gather.1
  132.7 48.8 all-reduce.3

commit v2 on v1

--- a/solution.py
+++ b/solution.py
@@ -32,7 +32,11 @@
     return me // 2, me % 2
 
 
-def enter(chip, core):
+PANELS = 10
+LAYERS = 4
+
+
+def enter(chip, core, layers=False):
     barrier = pltpu.get_barrier_semaphore()
 
     def greet(step, carry):
@@ -42,183 +46,448 @@
 
     lax.fori_loop(1, CHIPS, greet, 0)
     pl.semaphore_signal(barrier, inc=1, device_id={"seq": 2 * chip + 1 - core}, device_id_type=MESH)
-    pl.semaphore_wait(barrier, CHIPS)
-
-
-def remote(src, dst, send_sem, recv_sem, device):
+    if layers:
+        layer = lax.axis_index("head")
+        for step in (1, LAYERS - 1):
+            pl.semaphore_signal(
+                barrier, inc=1, device_id={"head": (layer + step) % LAYERS}, device_id_type=MESH
+            )
+    pl.semaphore_wait(barrier, CHIPS + (2 if layers else 0))
+
+
+def remote(src, dst, send_sem, recv_sem, device, axis="seq"):
     return pltpu.make_async_remote_copy(
         src_ref=src,
         dst_ref=dst,
         send_sem=send_sem,
         recv_sem=recv_sem,
-        device_id={"seq": device},
+        device_id={axis: device},
         device_id_type=MESH,
     )
 
 
-def deal_kernel(kv_ref, q_ref, kv_out, q_out, kv_send, kv_recv, pass_send, pass_recv, q_send, q_recv):
-    chip, core = place()
-    partner = 2 * chip + 1 - core
+def deal_queries(chip, core, src, dst, send, recv):
     third = third_of(chip)
     slot = chip - start_of(third)
-    enter(chip, core)
-
-    def kv_copy(d):
-        return remote(
-            kv_ref.at[:, d // 3], kv_out.at[:, chip, core], kv_send.at[d], kv_recv.at[chip], 2 * d + core
-        )
-
-    def q_copy(h):
-        return remote(q_ref.at[:, h], q_out.at[:, slot], q_send.at[h], q_recv.at[slot], 2 * (3 * h + third) + core)
-
-    def own_kv():
-        return pltpu.make_async_copy(kv_ref.at[:, chip // 3], kv_out.at[:, chip, core], kv_recv.at[chip])
-
-    def own_q():
-        return pltpu.make_async_copy(q_ref.at[:, chip // 3], q_out.at[:, slot], q_recv.at[slot])
-
-    def send_q(h, carry):
-        @pl.when(3 * h + third != chip)
-        def _():
-            q_copy(h).start()
-
-        @pl.when(3 * h + third == chip)
-        def _():
-            own_q().start()
-
-        return carry
-
-    def send_kv(step, carry):
-        d = (chip + step) % CHIPS
-
-        @pl.when(jnp.logical_and(d < BUSY, step > 0))
-        def _():
-            kv_copy(d).start()
-
-        @pl.when(jnp.logical_and(d < BUSY, step == 0))
-        def _():
-            own_kv().start()
-
-        return carry
-
-    lax.fori_loop(0, CHIPS, send_kv, 0)
-    lax.fori_loop(0, HEADS, send_q, 0)
-
     own_third = chip % 3
     first = start_of(own_third)
     count = start_of(own_third + 1) - first
-
-    def pass_copy(source):
+    partner = 2 * chip + 1 - core
+
+    def copy(h):
+        return remote(src.at[h], dst.at[slot], send.at[h], recv.at[slot], 2 * (3 * h + third) + core)
+
+    def own():
+        return pltpu.make_async_copy(src.at[chip // 3], dst.at[slot], recv.at[slot])
+
+    def begin():
+        def go(h, carry):
+            @pl.when(3 * h + third != chip)
+            def _():
+                copy(h).start()
+
+            @pl.when(3 * h + third == chip)
+            def _():
+                own().start()
+
+            return carry
+
+        lax.fori_loop(0, HEADS, go, 0)
+
+    def arrived():
+        @pl.when(chip < BUSY)
+        def _():
+            def come(n, carry):
+                @pl.when(first + n != chip)
+                def _():
+                    remote(src.at[0], dst.at[n], send.at[0], recv.at[n], partner).wait_recv()
+
+                @pl.when(first + n == chip)
+                def _():
+                    own().wait()
+
+                return carry
+
+            lax.fori_loop(0, count, come, 0)
+
+            @pl.when(count < SLOTS)
+            def _():
+                dst[SLOTS - 1] = jnp.zeros_like(dst[SLOTS - 1])
+
+    def sent():
+        def gone(h, carry):
+            @pl.when(3 * h + third != chip)
+            def _():
+                copy(h).wait_send()
+
+            return carry
+
+        lax.fori_loop(0, HEADS, gone, 0)
+
+    return begin, arrived, sent
+
+
+def deal_keys(chip, core, src, dst, kv_send, kv_recv, pass_send, pass_recv):
+    partner = 2 * chip + 1 - core
+
+    def copy(d):
+        return remote(src.at[:, d // 3], dst.at[:, chip, core], kv_send.at[d], kv_recv.at[chip], 2 * d + core)
+
+    def own():
+        return pltpu.make_async_copy(src.at[:, chip // 3], dst.at[:, chip, core], kv_recv.at[chip])
+
+    def pass_copy(source, half):
         return remote(
-            kv_out.at[:, source, core],
-            kv_out.at[:, source, core],
-            pass_send.at[source],
-            pass_recv.at[source],
-            partner,
+            dst.at[:, source, half], dst.at[:, source, half], pass_send.at[source], pass_recv.at[source], partner
         )
 
-    def pass_wait(source):
+    def begin():
+        def go(step, carry):
+            d = (chip + step) % CHIPS
+
+            @pl.when(jnp.logical_and(d < BUSY, step > 0))
+            def _():
+                copy(d).start()
+
+            @pl.when(jnp.logical_and(d < BUSY, step == 0))
+            def _():
+                own().start()
+
+            return carry
+
+        lax.fori_loop(0, CHIPS, go, 0)
+
+    def arrived():
+        @pl.when(chip < BUSY)
+        def _():
+            def come(step, carry):
+                source = (chip + CHIPS - step) % CHIPS
+
+                @pl.when(step > 0)
+                def _():
+                    remote(
+                        src.at[:, 0], dst.at[:, source, core], kv_send.at[0], kv_recv.at[source], partner
+                    ).wait_recv()
+
+                @pl.when(step == 0)
+                def _():
+                    own().wait()
+
+                pass_copy(source, core).start()
+                return carry
+
+            lax.fori_loop(0, CHIPS, come, 0)
+
+            def passed(step, carry):
+                source = (chip + CHIPS - step) % CHIPS
+                pass_copy(source, 1 - core).wait_recv()
+                pass_copy(source, core).wait_send()
+                return carry
+
+            lax.fori_loop(0, CHIPS, passed, 0)
+
+    def sent():
+        def gone(step, carry):
+            d = (chip + step) % CHIPS
+
+            @pl.when(d < BUSY)
+            def _():
+                copy(d).wait_send()
+
+            return carry
+
+        lax.fori_loop(1, CHIPS, gone, 0)
+
+    return begin, arrived, sent
+
+
+VMEM = pl.BlockSpec(memory_space=pltpu.VMEM)
+HBM = pl.BlockSpec(memory_space=pl.ANY)
+DMA = pltpu.SemaphoreType.DMA
+
+
+class Gather:
+    def __init__(self, rows_ref, own_send, pass_send, recv):
+        self.ref, self.own_send, self.pass_send, self.recv = rows_ref, own_send, pass_send, recv
+        self.layer = lax.axis_index("head")
+        self.right, self.left = (self.layer + 1) % LAYERS, (self.layer + LAYERS - 1) % LAYERS
+        self.across = (self.layer + 2) % LAYERS
+        self.height = rows_ref.shape[0] // LAYERS
+        self.width = rows_ref.shape[1] // PANELS
+
+    def rows(self, layer):
+        return pl.ds(pl.multiple_of(layer * self.height, self.height), self.height)
+
+    def columns(self, panel):
+        return pl.ds(panel * self.width, self.width)
+
+    def block(self, layer, panel):
+        return self.ref.at[self.rows(layer), self.columns(panel)]
+
+    def copy(self, layer, panel, send, kind, target):
+        block = self.block(layer, panel)
+        return remote(block, block, send, self.recv.at[kind, panel], target, "head")
+
+    def own(self, panel):
+        return (
+            self.copy(self.layer, panel, self.own_send.at[0, panel], 0, self.right),
+            self.copy(self.layer, panel, self.own_send.at[1, panel], 1, self.left),
+        )
+
+    def start(self, panel):
+        for copy in self.own(panel):
+            copy.start()
+
+    def passing(self, panel):
+        if panel % 2 == 0:
+            return self.copy(self.left, panel, self.pass_send.at[panel], 2, self.right)
+        return self.copy(self.right, panel, self.pass_send.at[panel], 2, self.left)
+
+    def relay(self, panel):
+        if panel % 2 == 0:
+            self.copy(self.left, panel, self.pass_send.at[panel], 0, self.right).wait_recv()
+        else:
+            self.copy(self.right, panel, self.pass_send.at[panel], 1, self.left).wait_recv()
+        self.passing(panel).start()
+
+    def rest(self, panel):
+        if panel % 2 == 0:
+            self.copy(self.right, panel, self.pass_send.at[panel], 1, self.left).wait_recv()
+        else:
+            self.copy(self.left, panel, self.pass_send.at[panel], 0, self.right).wait_recv()
+        self.copy(self.across, panel, self.pass_send.at[panel], 2, self.right).wait_recv()
+
+    def sent(self):
+        for panel in range(PANELS):
+            for copy in self.own(panel):
+                copy.wait_send()
+            self.passing(panel).wait_send()
+
+
+GATHER_SEMS = [DMA((2, PANELS)), DMA((PANELS,)), DMA((3, PANELS))]
+DEAL_SEMS = [DMA((CHIPS,))] * 4
+QUERY_SEMS = [DMA((HEADS,)), DMA((SLOTS,))]
+
+
+def panel_of_w(w_hbm, w_ref, sems, panel):
+    depth = w_ref.shape[1] // PANELS
+    rows = pl.ds(panel * depth, depth)
+    return pltpu.make_async_copy(w_hbm.at[:, rows], w_ref.at[:, rows], sems.at[panel])
+
+
+def add_panel(totals, rows_ref, w_ref, panel, first):
+    depth = w_ref.shape[1] // PANELS
+    span = slice(panel * depth, (panel + 1) * depth)
+    for c in range(3):
+        term = jnp.dot(rows_ref[:, span], w_ref[c, span, :], preferred_element_type=jnp.float32)
+        totals[c] = term if first else totals[c] + term
+
+
+def split_heads(totals, q_heads, kv_heads):
+    for h in range(HEADS):
+        span = slice(h * HD, (h + 1) * HD)
+        q_heads[h] = totals[0, :, span].astype(jnp.bfloat16)
+        kv_heads[0, h] = totals[1, :, span].astype(jnp.bfloat16)
+        kv_heads[1, h] = totals[2, :, span].astype(jnp.bfloat16)
+
+
+def project_kernel(
+    x_ref, w_hbm, readout_ref, kv_out, q_out, r_out,
+    x_all, w_ref, totals, q_heads, kv_heads, r_heads, w_sems, *sems
+):
+    chip, core = place()
+    for panel in range(PANELS):
+        panel_of_w(w_hbm, w_ref, w_sems, panel).start()
+    gather = Gather(x_all, *sems[:3])
+    x_all[gather.rows(gather.layer), :] = x_ref[...]
+    for h in range(HEADS):
+        r_heads[h] = readout_ref[:, h * HD : (h + 1) * HD]
+    enter(chip, core, layers=True)
+    ahead = 3
+    for panel in range(ahead):
+        gather.start(panel)
+    r_begin, r_arrived, r_sent = deal_queries(chip, core, r_heads, r_out, *sems[3:5])
+    q_begin, q_arrived, q_sent = deal_queries(chip, core, q_heads, q_out, *sems[5:7])
+    kv_begin, kv_arrived, kv_sent = deal_keys(chip, core, kv_heads, kv_out, *sems[7:])
+    r_begin()
+
+    gather.relay(0)
+    for panel in range(PANELS):
+        if panel + ahead < PANELS:
+            gather.start(panel + ahead)
+        if panel + 1 < PANELS:
+            gather.relay(panel + 1)
+        gather.rest(panel)
+        panel_of_w(w_hbm, w_ref, w_sems, panel).wait()
+        add_panel(totals, x_all, w_ref, panel, panel == 0)
+    split_heads(totals, q_heads, kv_heads)
+    kv_begin()
+    q_begin()
+    kv_arrived()
+    q_arrived()
+    r_arrived()
+    gather.sent()
+    kv_sent()
+    q_sent()
+    r_sent()
+
+
+def project(x, w, readout, collective_id):
+    tokens, width = LAYERS * x.shape[0], x.shape[1]
+    block = jax.ShapeDtypeStruct((SLOTS, HD, HD), jnp.bfloat16)
+    return pl.pallas_call(
+        project_kernel,
+        out_shape=(jax.ShapeDtypeStruct((2, CHIPS, 2, HD, HD), jnp.bfloat16), block, block),
+        in_specs=[VMEM, HBM, VMEM],
+        out_specs=(VMEM, VMEM, VMEM),
+        scratch_shapes=[
+            pltpu.VMEM((tokens, width), jnp.bfloat16),
+            pltpu.VMEM(w.shape, jnp.bfloat16),
+            pltpu.VMEM((3, tokens, HEADS * HD), jnp.float32),
+            pltpu.VMEM((HEADS, HD, HD), jnp.bfloat16),
+            pltpu.VMEM((2, HEADS, HD, HD), jnp.bfloat16),
+            pltpu.VMEM((HEADS, HD, HD), jnp.bfloat16),
+            DMA((PANELS,)),
+        ]
+        + GATHER_SEMS
+        + QUERY_SEMS
+        + QUERY_SEMS
+        + DEAL_SEMS,
+        compiler_params=pltpu.CompilerParams(
+            collective_id=collective_id, has_side_effects=True, vmem_limit_bytes=48 << 20
+        ),
+        name="project",
+    )(x, w, readout)
+
+
+def input_grad_kernel(
+    q_grad, kv_grad, w_hbm, gx_ref, kv_out, q_out,
+    x_all, w_ref, totals, q_heads, kv_heads, grads, parts, via, direct, mixed, mix_out,
+    w_sems, via_send, via_recv, direct_send, direct_recv, mix_send, mix_recv, *sems
+):
+    chip, core = place()
+    for panel in range(PANELS):
+        panel_of_w(w_hbm, w_ref, w_sems, panel).start()
+    gather = Gather(x_all, *sems[:3])
+    for h in range(HEADS):
+        span = slice(h * HD, (h + 1) * HD)
+        grads[0, :, span] = q_grad[h]
+        grads[1, :, span] = kv_grad[0, h]
+        grads[2, :, span] = kv_grad[1, h]
+    enter(chip, core, layers=True)
+    q_begin, q_arrived, q_sent = deal_queries(chip, core, q_heads, q_out, *sems[3:5])
+    kv_begin, kv_arrived, kv_sent = deal_keys(chip, core, kv_heads, kv_out, *sems[5:])
+    depth = gather.width
+
+    def near_far(panel):
+        return (gather.right, gather.left) if panel % 2 == 0 else (gather.left, gather.right)
+
+    def part(layer, panel):
+        return parts.at[gather.rows(layer), gather.columns(panel)]
+
+    def piece(ref, panel):
+        return ref.at[:, gather.columns(panel)]
+
+    def via_copy(panel):
         return remote(
-            kv_out.at[:, source, 1 - core],
-            kv_out.at[:, source, 1 - core],
-            pass_send.at[source],
-            pass_recv.at[source],
-            partner,
+            part(gather.across, panel), piece(via, panel), via_send.at[panel], via_recv.at[panel],
+            near_far(panel)[1], "head",
         )
 
-    @pl.when(chip < BUSY)
-    def _():
-        def arrive(step, carry):
-            source = (chip + CHIPS - step) % CHIPS
-
-            @pl.when(step > 0)
-            def _():
-                remote(
-                    kv_ref.at[:, 0], kv_out.at[:, source, core], kv_send.at[0], kv_recv.at[source], partner
-                ).wait_recv()
-
-            @pl.when(step == 0)
-            def _():
-                own_kv().wait()
-
-            pass_copy(source).start()
-            return carry
-
-        lax.fori_loop(0, CHIPS, arrive, 0)
-
-        def arrive_q(n, carry):
-            @pl.when(first + n != chip)
-            def _():
-                remote(q_ref.at[:, 0], q_out.at[:, n], q_send.at[0], q_recv.at[n], partner).wait_recv()
-
-            @pl.when(first + n == chip)
-            def _():
-                own_q().wait()
-
-            return carry
-
-        lax.fori_loop(0, count, arrive_q, 0)
-
-        @pl.when(count < SLOTS)
-        def _():
-            q_out[:, SLOTS - 1] = jnp.zeros_like(q_out[:, SLOTS - 1])
-
-        def passed(step, carry):
-            source = (chip + CHIPS - step) % CHIPS
-            pass_wait(source).wait_recv()
-            pass_copy(source).wait_send()
-            return carry
-
-        lax.fori_loop(0, CHIPS, passed, 0)
-
-    def sent_kv(step, carry):
-        d = (chip + step) % CHIPS
-
-        @pl.when(d < BUSY)
-        def _():
-            kv_copy(d).wait_send()
-
-        return carry
-
-    lax.fori_loop(1, CHIPS, sent_kv, 0)
-
-    def sent_q(h, carry):
-        @pl.when(3 * h + third != chip)
-        def _():
-            q_copy(h).wait_send()
-
-        return carry
-
-    lax.fori_loop(0, HEADS, sent_q, 0)
-
-
-VMEM = pl.BlockSpec(memory_space=pltpu.VMEM)
-DMA = pltpu.SemaphoreType.DMA
-
-
-def deal(kv, q, collective_id):
-    parts = q.shape[0]
+    def direct_copy(panel):
+        target = near_far(panel)[0]
+        return remote(
+            part(target, panel), piece(direct, panel), direct_send.at[panel], direct_recv.at[panel], target, "head"
+        )
+
+    def mix_copy(panel):
+        return remote(
+            piece(mix_out, panel), piece(mixed, panel), mix_send.at[panel], mix_recv.at[panel],
+            near_far(panel)[1], "head",
+        )
+
+    def share(panel):
+        span = slice(panel * depth, (panel + 1) * depth)
+        panel_of_w(w_hbm, w_ref, w_sems, panel).wait()
+        total = nt(grads[0], w_ref[0, span, :])
+        total += nt(grads[1], w_ref[1, span, :])
+        total += nt(grads[2], w_ref[2, span, :])
+        parts[:, span] = total.astype(jnp.bfloat16)
+        via_copy(panel).start()
+        direct_copy(panel).start()
+
+    def mix(panel):
+        span = slice(panel * depth, (panel + 1) * depth)
+        via_copy(panel).wait_recv()
+        mine = parts[gather.rows(near_far(panel)[1]), span]
+        mix_out[:, span] = (via[:, span].astype(jnp.float32) + mine.astype(jnp.float32)).astype(jnp.bfloat16)
+        mix_copy(panel).start()
+
+    def settle(panel):
+        span = slice(panel * depth, (panel + 1) * depth)
+        direct_copy(panel).wait_recv()
+        mix_copy(panel).wait_recv()
+        mine = parts[gather.rows(gather.layer), span].astype(jnp.float32)
+        total = mine + direct[:, span].astype(jnp.float32) + mixed[:, span].astype(jnp.float32)
+        total = total.astype(jnp.bfloat16)
+        gx_ref[:, span] = total
+        x_all[gather.rows(gather.layer), span] = total
+        gather.start(panel)
+
+    def absorb(panel):
+        gather.rest(panel)
+        add_panel(totals, x_all, w_ref, panel, panel == 0)
+
+    stages = ((share, 0), (mix, 1), (settle, 3), (gather.relay, 4), (absorb, 6))
+    for step in range(PANELS + 6):
+        for stage, lag in stages:
+            if 0 <= step - lag < PANELS:
+                stage(step - lag)
+    split_heads(totals, q_heads, kv_heads)
+    kv_begin()
+    q_begin()
+    kv_arrived()
+    q_arrived()
+    gather.sent()
+    for panel in range(PANELS):
+        via_copy(panel).wait_send()
+        direct_copy(panel).wait_send()
+        mix_copy(panel).wait_send()
+    kv_sent()
+    q_sent()
+
+
+def input_grad(q_grad, kv_grad, w, collective_id):
+    tokens, width = HD, w.shape[1]
+    rows = tokens // LAYERS
     return pl.pallas_call(
-        deal_kernel,
+        input_grad_kernel,
         out_shape=(
+            jax.ShapeDtypeStruct((rows, width), jnp.bfloat16),
             jax.ShapeDtypeStruct((2, CHIPS, 2, HD, HD), jnp.bfloat16),
-            jax.ShapeDtypeStruct((parts, SLOTS, HD, HD), jnp.bfloat16),
+            jax.ShapeDtypeStruct((SLOTS, HD, HD), jnp.bfloat16),
         ),
-        in_specs=[VMEM] * 2,
-        out_specs=(VMEM, VMEM),
+        in_specs=[VMEM, VMEM, HBM],
+        out_specs=(VMEM, VMEM, VMEM),
         scratch_shapes=[
-            DMA((CHIPS,)),
-            DMA((CHIPS,)),
-            DMA((CHIPS,)),
-            DMA((CHIPS,)),
-            DMA((HEADS,)),
-            DMA((SLOTS,)),
-        ],
+            pltpu.VMEM((tokens, width), jnp.bfloat16),
+            pltpu.VMEM(w.shape, jnp.bfloat16),
+            pltpu.VMEM((3, tokens, HEADS * HD), jnp.float32),
+            pltpu.VMEM((HEADS, HD, HD), jnp.bfloat16),
+            pltpu.VMEM((2, HEADS, HD, HD), jnp.bfloat16),
+            pltpu.VMEM((3, tokens, HEADS * HD), jnp.bfloat16),
+            pltpu.VMEM((tokens, width), jnp.bfloat16),
+        ]
+        + [pltpu.VMEM((rows, width), jnp.bfloat16)] * 4
+        + [DMA((PANELS,))] * 7
+        + GATHER_SEMS
+        + QUERY_SEMS
+        + DEAL_SEMS,
         compiler_params=pltpu.CompilerParams(
-            collective_id=collective_id, has_side_effects=True, vmem_limit_bytes=32 << 20
+            collective_id=collective_id, has_side_effects=True, vmem_limit_bytes=48 << 20
         ),
-        name="deal",
-    )(kv, q)
+        name="input_grad",
+    )(q_grad, kv_grad, w)
 
 
 def give_back(chip, core, src, dst, send, recv):
@@ -441,10 +710,10 @@
     return pl.ds(pl.multiple_of(chunk * CHUNK, CHUNK), CHUNK)
 
 
-def grads_kernel(kv_ref, qr_ref, key_hot, row_bar, dkv_ref, dq_ref, norm_ref, k_wide, q_wide, dq_acc):
+def grads_kernel(kv_ref, q_ref, r_ref, key_hot, row_bar, dkv_ref, dq_ref, norm_ref, k_wide, q_wide, dq_acc):
     k_wide[:, :HD] = kv_ref[0]
     k_wide[:, HD:] = key_hot[...]
-    q_wide[:, :HD] = qr_ref[0]
+    q_wide[:, :HD] = q_ref[...]
     q_wide[:, HD:] = row_bar[...]
     factor = SCALE * LOG2E
 
@@ -452,7 +721,7 @@
         top, total, weighted = carry
         rows = rows_of(chunk)
         raw = nt(k_wide[rows, :], q_wide[...])
-        dots = nt(kv_ref[1, rows, :], qr_ref[1])
+        dots = nt(kv_ref[1, rows, :], r_ref[...])
         new_top = jnp.maximum(top, raw.max(axis=0, keepdims=True))
         weights = jnp.exp2((raw - new_top) * factor)
         shrink = jnp.exp2((top - new_top) * factor)
@@ -474,11 +743,11 @@
     def grads(chunk, carry):
         rows = rows_of(chunk)
         raw = nt(k_wide[rows, :], q_wide[...])
-        dots = nt(kv_ref[1, rows, :], qr_ref[1])
+        dots = nt(kv_ref[1, rows, :], r_ref[...])
         weights = jnp.exp2(raw * factor - norm)
         slopes = (weights * (dots - row_dots)).astype(jnp.bfloat16)
-        dkv_ref[0, rows, :] = (SCALE * nn(slopes, qr_ref[0])).astype(jnp.bfloat16)
-        dkv_ref[1, rows, :] = nn(weights.astype(jnp.bfloat16), qr_ref[1]).astype(jnp.bfloat16)
+        dkv_ref[0, rows, :] = (SCALE * nn(slopes, q_ref[...])).astype(jnp.bfloat16)
+        dkv_ref[1, rows, :] = nn(weights.astype(jnp.bfloat16), r_ref[...]).astype(jnp.bfloat16)
         dq_acc[...] += tn(kv_ref[0, rows, :], slopes)
         return carry
 
@@ -486,7 +755,7 @@
     dq_ref[...] = (SCALE * dq_acc[...]).T.astype(jnp.bfloat16)
 
 
-def attention_grads(kv, qr, key_hot, row_bar):
+def attention_grads(kv, q, r, key_hot, row_bar):
     return pl.pallas_call(
         grads_kernel,
         out_shape=(
@@ -494,7 +763,7 @@
             jax.ShapeDtypeStruct((ROWS, HD), jnp.bfloat16),
             jax.ShapeDtypeStruct((1, ROWS), jnp.float32),
         ),
-        in_specs=[VMEM] * 4,
+        in_specs=[VMEM] * 5,
         out_specs=(VMEM, VMEM, VMEM),
         scratch_shapes=[
             pltpu.VMEM((TOKENS, 2 * HD), jnp.bfloat16),
@@ -503,7 +772,7 @@
         ],
         compiler_params=pltpu.CompilerParams(vmem_limit_bytes=48 << 20),
         name="attention_grads",
-    )(kv, qr, key_hot, row_bar)
+    )(kv, q, r, key_hot, row_bar)
 
 
 def tangent_kernel(
@@ -574,10 +843,6 @@
     return key_hot, row_bar
 
 
-def by_head(rows):
-    return jnp.swapaxes(rows.reshape(rows.shape[:-1] + (HEADS, HD)), -3, -2)
-
-
 def to_rows(heads):
     swapped = jnp.swapaxes(heads, -3, -2)
     return swapped.reshape(swapped.shape[:-2] + (HEADS * HD,))
@@ -585,30 +850,16 @@
 
 def on_device(clip_tokens, w_qkv, readout, token_latent_frame, frame_mask):
     key_hot, row_bar = mask_sides(token_latent_frame, frame_mask)
-    tokens_all = lax.all_gather(clip_tokens, "head", axis=0, tiled=True)
-    projected = jnp.einsum(
-        "td,cde->cte", tokens_all, w_qkv, preferred_element_type=jnp.float32
-    ).astype(jnp.bfloat16)
-    heads = by_head(projected)
-    kv, qr = deal(heads[1:], jnp.stack([heads[0], by_head(readout)]), 0)
+    kv, q, r = project(clip_tokens, w_qkv, readout, 0)
     kv = kv.reshape(2, TOKENS, HD)
-    qr = qr.reshape(2, ROWS, HD)
-    dkv, dq, norm = attention_grads(kv, qr, key_hot, row_bar)
+    q = q.reshape(ROWS, HD)
+    dkv, dq, norm = attention_grads(kv, q, r.reshape(ROWS, HD), key_hot, row_bar)
     kv_grad, q_grad = reduce_back(
         dkv.reshape(2, CHIPS, 2, HD, HD), dq.reshape(SLOTS, HD, HD), 1
     )
-    grads = to_rows(jnp.concatenate([q_grad[None], kv_grad]))
-    partial_input = jnp.einsum("cte,cde->td", grads, w_qkv, preferred_element_type=jnp.float32)
-    input_sum = lax.psum(partial_input.astype(jnp.bfloat16), "head")
-    panel_rows = clip_tokens.shape[0]
-    grad_x = lax.dynamic_slice_in_dim(input_sum, lax.axis_index("head") * panel_rows, panel_rows)
-    tangents = jnp.einsum(
-        "td,cde->cte", input_sum, w_qkv, preferred_element_type=jnp.float32
-    ).astype(jnp.bfloat16)
-    dot_heads = by_head(tangents)
-    kv_dot, q_dot = deal(dot_heads[1:], dot_heads[:1], 2)
+    grad_x, kv_dot, q_dot = input_grad(q_grad, kv_grad, w_qkv, 2)
     out = attention_tangent(
-        kv, qr[0], kv_dot.reshape(2, TOKENS, HD), q_dot.reshape(ROWS, HD), key_hot, row_bar, norm
+        kv, q, kv_dot.reshape(2, TOKENS, HD), q_dot.reshape(ROWS, HD), key_hot, row_bar, norm
     )
     penalty_grad = to_rows(return_queries(out.reshape(SLOTS, HD, HD), 3))
     return (grad_x, penalty_grad)

time: 254 us -> 179 us (0.70)
  waiting for transfers between devices: 71.2 us -> 0 us
  Pallas kernels: 114 us -> 169 us
  matrix products: 35.3 us -> 0.29 us
  between operations: 14.2 us -> 0.76 us
  local copies, waits for them, and re-layouts: 15.3 us -> 4.92 us
    pallas_call x2, Pallas kernels: 48.5 us -> 103 us  [the longest x1 55.5 us: input_grad(): pl.pallas_call(input_grad_kernel, out_shape=(jax.ShapeDtypeStruct((rows,...]
    psum x1 -> x0, waiting for transfers between devices: 48.3 us -> none  [on_device(): input_sum = lax.psum(partial_input.astype(jnp.bfloat16), 'head')]
    dot_general x3 -> x0, matrix products: 34.3 us -> none  [the longest x1 12.2 us: on_device(): jnp.einsum('td,cde->cte', tokens_all, w_qkv, preferred_element_type=jnp.f...]
    all_gather x1 -> x0, waiting for transfers between devices: 22.2 us -> none  [on_device(): tokens_all = lax.all_gather(clip_tokens, 'head', axis=0, tiled=True)]
    slice x5 -> x0, local copies, waits for them, and re-layouts: 2.65 us -> none  [the longest x2 1.92 us: on_device(): kv_dot, q_dot = deal(dot_heads[1:], dot_heads[:1], 2)]
  transfers between devices with their start and end apart: 2 -> 0, of which waited for: 2 -> 0; matrix products, arithmetic and copies ran while one was open for 3% -> 0% of each run, Pallas kernels for 0% -> 0%
where the time goes in v2:
time: 179 us; the launch traced here: 178 us
  Pallas kernels  169 us (94%)
  local copies, waits for them, and re-layouts  4.92 us (3%)
  other arithmetic  3.19 us (2%)
    pallas_call x1, Pallas kernels, input_grad(): pl.pallas_call(input_grad_kernel, out_shape=(jax.ShapeDtypeStruct((rows,...  55.5 us
    pallas_call x1, Pallas kernels, project(): pl.pallas_call(project_kernel, out_shape=(jax.ShapeDtypeStruct((2, CHIPS,...  47.4 us
    pallas_call x1, Pallas kernels, reduce_back(): pl.pallas_call(reduce_kernel, out_shape=(jax.ShapeDtypeStruct((2, HEADS,...  24.3 us
    pallas_call x1, Pallas kernels, attention_grads(): pl.pallas_call(grads_kernel, out_shape=(jax.ShapeDtypeStruct((2, TOKENS,...  19.1 us
    pallas_call x1, Pallas kernels, attention_tangent(): pl.pallas_call(tangent_kernel, out_shape=jax.ShapeDtypeStruct((ROWS, HD),...  12.7 us
    pallas_call x1, Pallas kernels, return_queries(): pl.pallas_call(return_kernel, out_shape=jax.ShapeDtypeStruct((HEADS, HD,...  9.98 us

profile of v2, /device:TPU:24, one launch (start us, length us, event | category | flops | bytes accessed | tf_op | source)
XLA Modules:
  0.0 178.2 jit_solution(1114090225351801088)
XLA Ops:
  0.7 0.7 compare_select_fusion
  1.4 1.3 gather_fusion
  2.7 0.3 fusion.1.row_bar
  3.0 2.5 %fusion.key_hot = bf16[4096,128]{1,0:T(8,128)(2,1)S(1)} fusion(s32[4096]{0:T(1024)} %param.8), kind=kLoop, calls=%fused_computation.2 | loop fusion | flops 1048576 | bytes 1064960 | tf_op jit(solution)/shard_map/convert_element_type | solution.py:834
  5.5 0.0 copy-start
  5.5 1.0 copy-done
  6.5 0.0 copy-start.1
  6.5 0.9 copy-done.1
  7.4 47.4 %project.1 = (bf16[2,16,2,128,128]{4,3,2,1,0:T(8,128)(2,1)S(1)}, bf16[6,128,128]{2,1,0:T(8,128)(2,1)S(1)}, bf16[6,128,128]{2,1,0:T(8,128)(2,1)S(1)}) custom-call(bf16[32,5120]{1,0:T(8,128)(2,1)S(1)} %copy-done, bf16[3,5120,640]{2,1,0:T(8,128)(2,1)} %w_hbm.3, bf16[128,640]{1,0:T(8,128)(2,1)S(1)} %copy-done.1), custom_call_target="tpu_custom_call" | custom-call | tf_op jit(solution)/shard_map/project/pallas_call | solution.py:338
  54.8 19.1 %attention_grads.1 = (bf16[2,4096,128]{2,1,0:T(8,128)(2,1)S(1)}, bf16[768,128]{1,0:T(8,128)(2,1)S(1)}, f32[1,768]{1,0:T(1,128)S(1)}) custom-call(bf16[2,4096,128]{2,1,0:T(8,128)(2,1)S(1)} %bitcast.14, bf16[768,128]{1,0:T(8,128)(2,1)S(1)} %bitcast.18, bf16[768,128]{1,0:T(8,128)(2,1)S(1)} %bitcast.23, bf16[4096,128]{1,0:T(8,128)(2,1)S(1)} %fusion.key_hot, ...), custom_call_target="tpu_custom_call" | custom-call | tf_op jit(solution)/shard_map/attention_grads/pallas_call | solution.py:759
  73.9 24.3 %reduce_back.1 = (bf16[2,5,128,128]{3,2,1,0:T(8,128)(2,1)S(1)}, bf16[5,128,128]{2,1,0:T(8,128)(2,1)S(1)}) custom-call(bf16[2,16,2,128,128]{4,3,2,1,0:T(8,128)(2,1)S(1)} %bitcast.17, bf16[6,128,128]{2,1,0:T(8,128)(2,1)S(1)} %bitcast.24), custom_call_target="tpu_custom_call" | custom-call | tf_op jit(solution)/shard_map/reduce_back/pallas_call | solution.py:665
  98.2 55.5 %input_grad.1 = (bf16[32,5120]{1,0:T(8,128)(2,1)S(1)}, bf16[2,16,2,128,128]{4,3,2,1,0:T(8,128)(2,1)S(1)}, bf16[6,128,128]{2,1,0:T(8,128)(2,1)S(1)}) custom-call(bf16[5,128,128]{2,1,0:T(8,128)(2,1)S(1)} %get-tuple-element.18.q_grad, bf16[2,5,128,128]{3,2,1,0:T(8,128)(2,1)S(1)} %get-tuple-element.19.kv_grad, bf16[3,5120,640]{2,1,0:T(8,128)(2,1)} %w_hbm.3), custom_call_target="tpu_custom_call" | custom-call | tf_op jit(solution)/shard_map/input_grad/pallas_call | solution.py:463
  153.8 12.7 %attention_tangent.1 = bf16[768,128]{1,0:T(8,128)(2,1)S(1)} custom-call(bf16[2,4096,128]{2,1,0:T(8,128)(2,1)S(1)} %bitcast.15, bf16[768,128]{1,0:T(8,128)(2,1)S(1)} %bitcast.19, bf16[2,4096,128]{2,1,0:T(8,128)(2,1)S(1)} %bitcast.16, bf16[768,128]{1,0:T(8,128)(2,1)S(1)} %bitcast.22, bf16[4096,128]{1,0:T(8,128)(2,1)S(1)} %fusion.key_hot, ...), custom_call_target="tpu_custom_call" | custom-call | tf_op jit(solution)/shard_map/attention_tangent/pallas_call | solution.py:812
  166.5 10.0 %return_queries.1 = bf16[5,128,128]{2,1,0:T(8,128)(2,1)S(1)} custom-call(bf16[6,128,128]{2,1,0:T(8,128)(2,1)S(1)} %bitcast.20), custom_call_target="tpu_custom_call" | custom-call | tf_op jit(solution)/shard_map/return_queries/pallas_call | solution.py:559
  176.5 0.2 copy.7
  176.7 0.8 copy.8
  177.5 0.7 copy.10
  (1 shorter events, 0.0 us)
Async XLA Ops:
  5.5 1.0 copy-start
  6.5 0.9 copy-start.1

commit v3 on v0

v3 whole, which is shorter than its diff:
```python
import functools
import math

import jax
import jax.numpy as jnp
from jax import lax
from jax.experimental import pallas as pl
from jax.experimental.pallas import tpu as pltpu
from jax.sharding import PartitionSpec as P

HD = 128
MESH = pl.DeviceIdType.MESH
LOG2E = math.log2(math.e)
BARRED = -1e30

CHIPS = 16
BUSY = 15
HEADS = 5
SLOTS = 6
LAG = 2


def start_of(third):
    return (CHIPS * third + 2) // 3


def third_of(chip):
    return (chip * 3) // CHIPS


def place():
    me = lax.axis_index("seq")
    return me // 2, me % 2


PANELS = 10
LAYERS = 4


def enter(chip, core, layers=False):
    barrier = pltpu.get_barrier_semaphore()

    def greet(step, carry):
        peer = (chip + step) % CHIPS
        pl.semaphore_signal(barrier, inc=1, device_id={"seq": 2 * peer + core}, device_id_type=MESH)
        return carry

    lax.fori_loop(1, CHIPS, greet, 0)
    pl.semaphore_signal(barrier, inc=1, device_id={"seq": 2 * chip + 1 - core}, device_id_type=MESH)
    if layers:
        layer = lax.axis_index("head")
        for step in (1, LAYERS - 1):
            pl.semaphore_signal(
                barrier, inc=1, device_id={"head": (layer + step) % LAYERS}, device_id_type=MESH
            )
    pl.semaphore_wait(barrier, CHIPS + (2 if layers else 0))


def remote(src, dst, send_sem, recv_sem, device, axis="seq"):
    return pltpu.make_async_remote_copy(
        src_ref=src,
        dst_ref=dst,
        send_sem=send_sem,
        recv_sem=recv_sem,
        device_id={axis: device},
        device_id_type=MESH,
    )


def deal_queries(chip, core, src, dst, send, recv):
    third = third_of(chip)
    slot = chip - start_of(third)
    own_third = chip % 3
    first = start_of(own_third)
    count = start_of(own_third + 1) - first
    partner = 2 * chip + 1 - core

    def copy(h):
        return remote(src.at[h], dst.at[slot], send.at[h], recv.at[slot], 2 * (3 * h + third) + core)

    def own():
        return pltpu.make_async_copy(src.at[chip // 3], dst.at[slot], recv.at[slot])

    def begin():
        def go(h, carry):
            @pl.when(3 * h + third != chip)
            def _():
                copy(h).start()

            @pl.when(3 * h + third == chip)
            def _():
                own().start()

            return carry

        lax.fori_loop(0, HEADS, go, 0)

    def arrived():
        @pl.when(chip < BUSY)
        def _():
            def come(n, carry):
                @pl.when(first + n != chip)
                def _():
                    remote(src.at[0], dst.at[n], send.at[0], recv.at[n], partner).wait_recv()

                @pl.when(first + n == chip)
                def _():
                    own().wait()

                return carry

            lax.fori_loop(0, count, come, 0)

            @pl.when(count < SLOTS)
            def _():
                dst[SLOTS - 1] = jnp.zeros_like(dst[SLOTS - 1])

    def sent():
        def gone(h, carry):
            @pl.when(3 * h + third != chip)
            def _():
                copy(h).wait_send()

            return carry

        lax.fori_loop(0, HEADS, gone, 0)

    return begin, arrived, sent


def deal_keys(chip, core, src, dst, kv_send, kv_recv, pass_send, pass_recv):
    partner = 2 * chip + 1 - core

    def copy(d):
        return remote(src.at[:, d // 3], dst.at[:, chip, core], kv_send.at[d], kv_recv.at[chip], 2 * d + core)

    def own():
        return pltpu.make_async_copy(src.at[:, chip // 3], dst.at[:, chip, core], kv_recv.at[chip])

    def pass_copy(source, half):
        return remote(
            dst.at[:, source, half], dst.at[:, source, half], pass_send.at[source], pass_recv.at[source], partner
        )

    def begin():
        def go(step, carry):
            d = (chip + step) % CHIPS

            @pl.when(jnp.logical_and(d < BUSY, step > 0))
            def _():
                copy(d).start()

            @pl.when(jnp.logical_and(d < BUSY, step == 0))
            def _():
                own().start()

            return carry

        lax.fori_loop(0, CHIPS, go, 0)

    def source_of(step):
        return (chip + CHIPS - step) % CHIPS

    def arrive(step):
        source = source_of(step)

        @pl.when(step > 0)
        def _():
            remote(
                src.at[:, 0], dst.at[:, source, core], kv_send.at[0], kv_recv.at[source], partner
            ).wait_recv()

        @pl.when(step == 0)
        def _():
            own().wait()

        pass_copy(source, core).start()

    def use(step, body):
        source = source_of(step)
        pass_copy(source, 1 - core).wait_recv()
        body(source)

    def consume(body):
        @pl.when(chip < BUSY)
        def _():
            def first(step, carry):
                arrive(step)
                return carry

            def both(step, carry):
                arrive(step)
                use(step - LAG, body)
                return carry

            def last(step, carry):
                use(step, body)
                return carry

            lax.fori_loop(0, LAG, first, 0)
            lax.fori_loop(LAG, CHIPS, both, 0)
            lax.fori_loop(CHIPS - LAG, CHIPS, last, 0)

    def sent():
        @pl.when(chip < BUSY)
        def _():
            def passed(step, carry):
                pass_copy(source_of(step), core).wait_send()
                return carry

            lax.fori_loop(0, CHIPS, passed, 0)

        def gone(step, carry):
            d = (chip + step) % CHIPS

            @pl.when(d < BUSY)
            def _():
                copy(d).wait_send()

            return carry

        lax.fori_loop(1, CHIPS, gone, 0)

    return begin, consume, sent


VMEM = pl.BlockSpec(memory_space=pltpu.VMEM)
HBM = pl.BlockSpec(memory_space=pl.ANY)
DMA = pltpu.SemaphoreType.DMA


class Gather:
    def __init__(self, rows_ref, own_send, pass_send, recv):
        self.ref, self.own_send, self.pass_send, self.recv = rows_ref, own_send, pass_send, recv
        self.layer = lax.axis_index("head")
        self.right, self.left = (self.layer + 1) % LAYERS, (self.layer + LAYERS - 1) % LAYERS
        self.across = (self.layer + 2) % LAYERS
        self.height = rows_ref.shape[0] // LAYERS
        self.width = rows_ref.shape[1] // PANELS

    def rows(self, layer):
        return pl.ds(pl.multiple_of(layer * self.height, self.height), self.height)

    def columns(self, panel):
        return pl.ds(panel * self.width, self.width)

    def block(self, layer, panel):
        return self.ref.at[self.rows(layer), self.columns(panel)]

    def copy(self, layer, panel, send, kind, target):
        block = self.block(layer, panel)
        return remote(block, block, send, self.recv.at[kind, panel], target, "head")

    def own(self, panel):
        return (
            self.copy(self.layer, panel, self.own_send.at[0, panel], 0, self.right),
            self.copy(self.layer, panel, self.own_send.at[1, panel], 1, self.left),
        )

    def start(self, panel):
        for copy in self.own(panel):
            copy.start()

    def passing(self, panel):
        if panel % 2 == 0:
            return self.copy(self.left, panel, self.pass_send.at[panel], 2, self.right)
        return self.copy(self.right, panel, self.pass_send.at[panel], 2, self.left)

    def relay(self, panel):
        if panel % 2 == 0:
            self.copy(self.left, panel, self.pass_send.at[panel], 0, self.right).wait_recv()
        else:
            self.copy(self.right, panel, self.pass_send.at[panel], 1, self.left).wait_recv()
        self.passing(panel).start()

    def rest(self, panel):
        if panel % 2 == 0:
            self.copy(self.right, panel, self.pass_send.at[panel], 1, self.left).wait_recv()
        else:
            self.copy(self.left, panel, self.pass_send.at[panel], 0, self.right).wait_recv()
        self.copy(self.across, panel, self.pass_send.at[panel], 2, self.right).wait_recv()

    def sent(self):
        for panel in range(PANELS):
            for copy in self.own(panel):
                copy.wait_send()
            self.passing(panel).wait_send()


def panel_of_w(w_hbm, w_ref, sems, panel):
    depth = w_ref.shape[1] // PANELS
    rows = pl.ds(panel * depth, depth)
    return pltpu.make_async_copy(w_hbm.at[:, rows], w_ref.at[:, rows], sems.at[panel])


def add_panel(totals, rows_ref, w_ref, panel, first):
    depth = w_ref.shape[1] // PANELS
    span = slice(panel * depth, (panel + 1) * depth)
    for c in range(3):
        term = jnp.dot(rows_ref[:, span], w_ref[c, span, :], preferred_element_type=jnp.float32)
        totals[c] = term if first else totals[c] + term


def split_heads(totals, q_heads, kv_heads):
    for h in range(HEADS):
        span = slice(h * HD, (h + 1) * HD)
        q_heads[h] = totals[0, :, span].astype(jnp.bfloat16)
        kv_heads[0, h] = totals[1, :, span].astype(jnp.bfloat16)
        kv_heads[1, h] = totals[2, :, span].astype(jnp.bfloat16)


def give_back(chip, core, src, dst, send, recv):
    own_third = chip % 3
    first = start_of(own_third)
    count = start_of(own_third + 1) - first
    third = third_of(chip)
    own_head = chip // 3

    def out_copy(n):
        return remote(src.at[n], dst.at[own_head], send.at[n], recv.at[own_head], 2 * (first + n) + core)

    def own():
        return pltpu.make_async_copy(src.at[chip - first], dst.at[own_head], recv.at[own_head])

    def begin():
        @pl.when(chip < BUSY)
        def _():
            def go(n, carry):
                @pl.when(first + n != chip)
                def _():
                    out_copy(n).start()

                @pl.when(first + n == chip)
                def _():
                    own().start()

                return carry

            lax.fori_loop(0, count, go, 0)

    def end():
        def come(h, carry):
            @pl.when(3 * h + third != chip)
            def _():
                remote(src.at[0], dst.at[h], send.at[0], recv.at[h], 2 * chip + 1 - core).wait_recv()

            @pl.when(3 * h + third == chip)
            def _():
                own().wait()

            return carry

        lax.fori_loop(0, HEADS, come, 0)

        @pl.when(chip < BUSY)
        def _():
            def gone(n, carry):
                @pl.when(first + n != chip)
                def _():
                    out_copy(n).wait_send()

                return carry

            lax.fori_loop(0, count, gone, 0)

    return begin, end


TOKENS = 4096
ROWS = SLOTS * HD
CHUNK = 2 * HD
SCALE = HD ** (-0.5)
FACTOR = SCALE * LOG2E


def nt(left, right):
    return lax.dot_general(left, right, (((1,), (1,)), ((), ())), preferred_element_type=jnp.float32)


def nn(left, right):
    return lax.dot_general(left, right, (((1,), (0,)), ((), ())), preferred_element_type=jnp.float32)


def tn(left, right):
    return lax.dot_general(left, right, (((0,), (0,)), ((), ())), preferred_element_type=jnp.float32)


def mask_sides(frames_ref, mask_ref, key_hot, row_bar, barred, first, core):
    frames = frames_ref[...]
    count = mask_ref.shape[0]
    lane = lax.broadcasted_iota(jnp.int32, (1, HD), 1)
    start = jnp.full((1, HD), TOKENS, jnp.int32)
    end = jnp.full((1, HD), TOKENS, jnp.int32)
    for f in range(count):
        below = jnp.sum((frames < f).astype(jnp.float32), keepdims=True).astype(jnp.int32)
        start = jnp.where(lane == f, below, start)
        end = jnp.where(lane == f - 1, below, end)

    def hot(tokens):
        return jnp.where(jnp.logical_and(tokens >= start, tokens < end), 1.0, 0.0).astype(jnp.bfloat16)

    row = lax.broadcasted_iota(jnp.int32, (HD, HD), 0)

    def fill(block, carry):
        key_hot[pl.ds(pl.multiple_of(block * HD, HD), HD), :] = hot(row + block * HD)
        return carry

    lax.fori_loop(0, TOKENS // HD, fill, 0)
    barred[...] = jnp.zeros_like(barred)
    barred[:count, :count] = jnp.where(mask_ref[...] == 1, 0.0, BARRED)
    table = barred[...].astype(jnp.bfloat16)
    for n in range(SLOTS):
        own = hot(row + (2 * (first + n) + core) * HD)
        row_bar[n * HD : (n + 1) * HD, :] = nn(own, table).astype(jnp.bfloat16)


TOP, TOTAL, WEIGHTED, NORM, ROW_DOTS, CURVE = range(6)


def whole_kernel(
    x_ref, w_hbm, readout_ref, frames_ref, mask_ref, gx_ref, pen_ref,
    w_ref, x_all, gx_all, totals, q_heads, kv_heads, r_heads, qd_heads, kvd_heads,
    kv, dots, q, r, qd, key_hot, row_bar, barred, stat,
    dkv, dq_acc, dq, penalty, other, summed, landed, q_landed, p_landed, plain, grads,
    parts, via, direct, mixed, mix_out,
    w_sems, *sems
):
    sems = list(sems)

    def take(n):
        taken = sems[:n]
        del sems[:n]
        return taken

    chip, core = place()
    partner = 2 * chip + 1 - core
    busy = chip < BUSY
    first = start_of(chip % 3)
    for panel in range(PANELS):
        panel_of_w(w_hbm, w_ref, w_sems, panel).start()
    gather = Gather(x_all, *take(3))
    x_all[gather.rows(gather.layer), :] = x_ref[...]
    for h in range(HEADS):
        r_heads[h] = readout_ref[:, h * HD : (h + 1) * HD]
    enter(chip, core, layers=True)
    ahead = 3
    for panel in range(ahead):
        gather.start(panel)
    r_begin, r_arrived, r_sent = deal_queries(chip, core, r_heads, r, *take(2))
    q_begin, q_arrived, q_sent = deal_queries(chip, core, q_heads, q, *take(2))
    kv_begin, kv_consume, kv_sent = deal_keys(chip, core, kv_heads, kv, *take(4))
    r_begin()
    mask_sides(frames_ref, mask_ref, key_hot, row_bar, barred, first, core)

    gather.relay(0)
    for panel in range(PANELS):
        if panel + ahead < PANELS:
            gather.start(panel + ahead)
        if panel + 1 < PANELS:
            gather.relay(panel + 1)
        gather.rest(panel)
        panel_of_w(w_hbm, w_ref, w_sems, panel).wait()
        add_panel(totals, x_all, w_ref, panel, panel == 0)
    split_heads(totals, q_heads, kv_heads)
    q_begin()
    kv_begin()

    def keys_of(array, source):
        return array[source].reshape(CHUNK, HD)

    def flat(array):
        return array[...].reshape(ROWS, HD)

    def logits(source):
        hot = key_hot[pl.ds(pl.multiple_of(source * CHUNK, CHUNK), CHUNK), :]
        return nt(
            jnp.concatenate([keys_of(kv.at[0], source), hot], axis=1),
            jnp.concatenate([flat(q), row_bar[...]], axis=1),
        )

    def stats(source):
        raw = logits(source)
        readout_dots = nt(keys_of(kv.at[1], source), flat(r))
        top = stat[TOP]
        new_top = jnp.maximum(top, raw.max(axis=0, keepdims=True))
        weights = jnp.exp2((raw - new_top) * FACTOR)
        shrink = jnp.exp2((top - new_top) * FACTOR)
        stat[TOP] = new_top
        stat[TOTAL] = stat[TOTAL] * shrink + weights.sum(axis=0, keepdims=True)
        stat[WEIGHTED] = stat[WEIGHTED] * shrink + (weights * readout_dots).sum(axis=0, keepdims=True)

    q_arrived()
    r_arrived()

    @pl.when(busy)
    def _():
        stat[...] = jnp.zeros_like(stat)
        stat[TOP] = jnp.full((1, ROWS), BARRED, jnp.float32)
        dq_acc[...] = jnp.zeros_like(dq_acc)

    kv_consume(stats)

    def swap(target):
        x_send, x_recv = swap_sems
        return remote(
            dkv.at[:, target, 1 - core], other.at[:, target], x_send.at[target], x_recv.at[target], partner
        )

    def out_copy(target):
        return remote(
            summed.at[:, target], landed.at[chip], sum_sems[0].at[target], sum_sems[1].at[chip], 2 * target + core
        )

    def own_sum():
        return pltpu.make_async_copy(summed.at[:, chip], landed.at[chip], sum_sems[1].at[chip])

    swap_sems = take(2)
    sum_sems = take(2)
    dq_begin, dq_end = give_back(chip, core, dq, q_landed, *take(2))

    def key_grads(step):
        target = (chip + step) % CHIPS
        weights = jnp.exp2(logits(target) * FACTOR - stat[NORM])
        readout_dots = nt(keys_of(kv.at[1], target), flat(r))
        slopes = (weights * (readout_dots - stat[ROW_DOTS])).astype(jnp.bfloat16)
        key_part = (SCALE * nn(slopes, flat(q))).astype(jnp.bfloat16)
        value_part = nn(weights.astype(jnp.bfloat16), flat(r)).astype(jnp.bfloat16)
        dkv[0, target] = key_part.reshape(2, HD, HD)
        dkv[1, target] = value_part.reshape(2, HD, HD)
        swap(target).start()
        dq_acc[...] += tn(keys_of(kv.at[0], target), slopes)

    def add_partner(step):
        target = (chip + step) % CHIPS
        swap(target).wait_recv()
        summed[:, target] = (
            dkv[:, target, core].astype(jnp.float32) + other[:, target].astype(jnp.float32)
        ).astype(jnp.bfloat16)

        @pl.when(step > 0)
        def _():
            out_copy(target).start()

        @pl.when(step == 0)
        def _():
            own_sum().start()

    @pl.when(busy)
    def _():
        stat[NORM] = stat[TOP] * FACTOR + jnp.log2(stat[TOTAL])
        stat[ROW_DOTS] = stat[WEIGHTED] / stat[TOTAL]
        key_grads(0)

        def go(step, carry):
            key_grads(step)
            add_partner(step - 1)
            return carry

        lax.fori_loop(1, CHIPS, go, 0)
        add_partner(CHIPS - 1)
        dq[...] = (SCALE * dq_acc[...]).T.astype(jnp.bfloat16).reshape(SLOTS, HD, HD)

    dq_begin()
    gather.sent()
    kv_sent()
    q_sent()
    r_sent()

    def come(step, carry):
        source = (chip + CHIPS - step) % CHIPS

        @pl.when(jnp.logical_and(source < BUSY, step > 0))
        def _():
            remote(
                summed.at[:, 0], landed.at[source], sum_sems[0].at[0], sum_sems[1].at[source], partner
            ).wait_recv()

        @pl.when(jnp.logical_and(source < BUSY, step == 0))
        def _():
            own_sum().wait()

        return carry

    lax.fori_loop(0, CHIPS, come, 0)
    for h in range(HEADS):
        span = slice(h * HD, (h + 1) * HD)
        total = landed[3 * h].astype(jnp.float32) + landed[3 * h + 1].astype(jnp.float32)
        total = (total + landed[3 * h + 2].astype(jnp.float32)).astype(jnp.bfloat16)
        grads[1, :, span] = total[0]
        grads[2, :, span] = total[1]
    dq_end()
    for h in range(HEADS):
        grads[0, :, h * HD : (h + 1) * HD] = q_landed[h]

    regather = Gather(gx_all, *take(3))
    qd_begin, qd_arrived, qd_sent = deal_queries(chip, core, qd_heads, qd, *take(2))
    kvd_begin, kvd_consume, kvd_sent = deal_keys(chip, core, kvd_heads, dots, *take(4))
    via_send, via_recv, direct_send, direct_recv, mix_send, mix_recv = take(6)
    depth = regather.width

    def near_far(panel):
        return (regather.right, regather.left) if panel % 2 == 0 else (regather.left, regather.right)

    def part(layer, panel):
        return parts.at[regather.rows(layer), regather.columns(panel)]

    def piece(ref, panel):
        return ref.at[:, regather.columns(panel)]

    def via_copy(panel):
        return remote(
            part(regather.across, panel), piece(via, panel), via_send.at[panel], via_recv.at[panel],
            near_far(panel)[1], "head",
        )

    def direct_copy(panel):
        target = near_far(panel)[0]
        return remote(
            part(target, panel), piece(direct, panel), direct_send.at[panel], direct_recv.at[panel], target, "head"
        )

    def mix_copy(panel):
        return remote(
            piece(mix_out, panel), piece(mixed, panel), mix_send.at[panel], mix_recv.at[panel],
            near_far(panel)[1], "head",
        )

    def share(panel):
        span = slice(panel * depth, (panel + 1) * depth)
        total = nt(grads[0], w_ref[0, span, :])
        total += nt(grads[1], w_ref[1, span, :])
        total += nt(grads[2], w_ref[2, span, :])
        parts[:, span] = total.astype(jnp.bfloat16)
        via_copy(panel).start()
        direct_copy(panel).start()

    def mix(panel):
        span = slice(panel * depth, (panel + 1) * depth)
        via_copy(panel).wait_recv()
        mine = parts[regather.rows(near_far(panel)[1]), span]
        mix_out[:, span] = (via[:, span].astype(jnp.float32) + mine.astype(jnp.float32)).astype(jnp.bfloat16)
        mix_copy(panel).start()

    def settle(panel):
        span = slice(panel * depth, (panel + 1) * depth)
        direct_copy(panel).wait_recv()
        mix_copy(panel).wait_recv()
        mine = parts[regather.rows(regather.layer), span].astype(jnp.float32)
        total = mine + direct[:, span].astype(jnp.float32) + mixed[:, span].astype(jnp.float32)
        total = total.astype(jnp.bfloat16)
        gx_ref[:, span] = total
        gx_all[regather.rows(regather.layer), span] = total
        regather.start(panel)

    def absorb(panel):
        regather.rest(panel)
        add_panel(totals, gx_all, w_ref, panel, panel == 0)

    stages = ((share, 0), (mix, 1), (settle, 3), (regather.relay, 4), (absorb, 6))
    for step in range(PANELS + 6):
        for stage, lag in stages:
            if 0 <= step - lag < PANELS:
                stage(step - lag)
    split_heads(totals, qd_heads, kvd_heads)
    qd_begin()
    kvd_begin()

    def tangent(source):
        keys, values = keys_of(kv.at[0], source), keys_of(kv.at[1], source)
        key_dots, value_dots = keys_of(dots.at[0], source), keys_of(dots.at[1], source)
        weights = jnp.exp2(logits(source) * FACTOR - stat[NORM])
        moved = nt(jnp.concatenate([keys, key_dots], axis=1), jnp.concatenate([flat(qd), flat(q)], axis=1))
        turned = weights * (moved * SCALE)
        dq_acc[...] += tn(values, turned.astype(jnp.bfloat16))
        plain[...] += tn(jnp.concatenate([values, value_dots], axis=1), weights.astype(jnp.bfloat16))
        stat[CURVE] += turned.sum(axis=0, keepdims=True)

    qd_arrived()

    @pl.when(busy)
    def _():
        dq_acc[...] = jnp.zeros_like(dq_acc)
        plain[...] = jnp.zeros_like(plain)

    kvd_consume(tangent)
    pen_begin, pen_end = give_back(chip, core, penalty, p_landed, *take(2))

    @pl.when(busy)
    def _():
        total = dq_acc[...] + plain[HD:, :] - stat[CURVE] * plain[:HD, :]
        penalty[...] = total.T.astype(jnp.bfloat16).reshape(SLOTS, HD, HD)

    pen_begin()

    @pl.when(busy)
    def _():
        def gone(step, carry):
            target = (chip + step) % CHIPS
            swap(target).wait_send()

            @pl.when(step > 0)
            def _():
                out_copy(target).wait_send()

            return carry

        lax.fori_loop(0, CHIPS, gone, 0)

    regather.sent()
    for panel in range(PANELS):
        via_copy(panel).wait_send()
        direct_copy(panel).wait_send()
        mix_copy(panel).wait_send()
    kvd_sent()
    qd_sent()
    pen_end()
    for h in range(HEADS):
        pen_ref[:, h * HD : (h + 1) * HD] = p_landed[h]


def on_device(clip_tokens, w_qkv, readout, token_latent_frame, frame_mask):
    panel_rows, width = clip_tokens.shape
    tokens, columns = readout.shape

    def low(*shape):
        return pltpu.VMEM(shape, jnp.bfloat16)

    def wide(*shape):
        return pltpu.VMEM(shape, jnp.float32)

    gather_sems = [DMA((2, PANELS)), DMA((PANELS,)), DMA((3, PANELS))]
    query_sems = [DMA((HEADS,)), DMA((SLOTS,))]
    back_sems = [DMA((SLOTS,)), DMA((HEADS,))]
    chip_sems = [DMA((CHIPS,))] * 4
    scratch = dict(
        w_ref=low(*w_qkv.shape),
        x_all=low(tokens, width),
        gx_all=low(tokens, width),
        totals=wide(3, tokens, columns),
        q_heads=low(HEADS, HD, HD),
        kv_heads=low(2, HEADS, HD, HD),
        r_heads=low(HEADS, HD, HD),
        qd_heads=low(HEADS, HD, HD),
        kvd_heads=low(2, HEADS, HD, HD),
        kv=low(2, CHIPS, 2, HD, HD),
        dots=low(2, CHIPS, 2, HD, HD),
        q=low(SLOTS, HD, HD),
        r=low(SLOTS, HD, HD),
        qd=low(SLOTS, HD, HD),
        key_hot=low(TOKENS, HD),
        row_bar=low(ROWS, HD),
        barred=wide(HD, HD),
        stat=wide(6, 1, ROWS),
        dkv=low(2, CHIPS, 2, HD, HD),
        dq_acc=wide(HD, ROWS),
        dq=low(SLOTS, HD, HD),
        penalty=low(SLOTS, HD, HD),
        other=low(2, CHIPS, HD, HD),
        summed=low(2, CHIPS, HD, HD),
        landed=low(CHIPS, 2, HD, HD),
        q_landed=low(HEADS, HD, HD),
        p_landed=low(HEADS, HD, HD),
        plain=wide(2 * HD, ROWS),
        grads=low(3, tokens, columns),
        parts=low(tokens, width),
        via=low(panel_rows, width),
        direct=low(panel_rows, width),
        mixed=low(panel_rows, width),
        mix_out=low(panel_rows, width),
        w_sems=DMA((PANELS,)),
    )
    sems = (
        gather_sems + query_sems * 2 + chip_sems + chip_sems + back_sems
        + gather_sems + query_sems + chip_sems + [DMA((PANELS,))] * 6 + back_sems
    )
    return pl.pallas_call(
        whole_kernel,
        out_shape=(
            jax.ShapeDtypeStruct((panel_rows, width), jnp.bfloat16),
            jax.ShapeDtypeStruct((tokens, columns), jnp.bfloat16),
        ),
        in_specs=[VMEM, HBM, VMEM, VMEM, VMEM],
        out_specs=(VMEM, VMEM),
        scratch_shapes=list(scratch.values()) + sems,
        compiler_params=pltpu.CompilerParams(
            collective_id=0, has_side_effects=True, vmem_limit_bytes=58 << 20
        ),
        name="whole",
    )(clip_tokens, w_qkv, readout, token_latent_frame.reshape(-1, HD), frame_mask)


def solution(mesh):
    return jax.shard_map(
        on_device,
        mesh=mesh,
        in_specs=(P(("seq", "head"), None), P(None, None, "head"), P("seq", "head"), P(), P()),
        out_specs=(P(("seq", "head"), None), P("seq", "head")),
        check_vma=False,
    )
```

time: 726 us -> 150 us (0.21); the launches traced: 714 us -> 149 us
  waiting for transfers between devices: 395 us -> 0 us
  matrix products: 190 us -> 0 us
  Pallas kernels: 0 us -> 145 us
  local copies, waits for them, and re-layouts: 110 us -> 3.31 us
  between operations: 14.6 us -> 0.64 us
    dot_general x132 -> x0, matrix products: 190 us -> none  [the longest x56 84.2 us: dots_of(): jnp.einsum('qhd,khd->hqk', left_side, right_side, preferred_element_type=...]
    all_gather x5 -> x0, waiting for transfers between devices: 183 us -> none  [the longest x1 49.7 us: on_device(): lax.all_gather(values_own, 'seq', axis=0, tiled=True)]
    reduce_scatter x2 -> x0, waiting for transfers between devices: 162 us -> none  [the longest x1 87.9 us: on_device(): lax.psum_scatter(value_parts.reshape(all_tokens, row_width).astype(jnp.bf...]
    pallas_call x0 -> x1, Pallas kernels: none -> 145 us  [on_device(): pl.pallas_call(whole_kernel, out_shape=(jax.ShapeDtypeStruct((panel_rows,...]
    unnamed x20 -> x2, local copies, waits for them, and re-layouts: 67.7 us -> 3.31 us
    psum x1 -> x0, waiting for transfers between devices: 47.9 us -> none  [on_device(): input_sum = lax.psum(partial_input.astype(jnp.bfloat16), 'head')]
    reshape x3 -> x0, local copies, waits for them, and re-layouts: 25.5 us -> none  [the longest x2 25.5 us: to_blocks(): return array.reshape(sub_count, sub_rows, head_count, HD)]
    convert_element_type x2 -> x0, local copies, waits for them, and re-layouts: 12.5 us -> none  [the longest x1 6.27 us: on_device(): key_parts.reshape(all_tokens, row_width).astype(jnp.bfloat16)]
  transfers between devices with their start and end apart: 8 -> 0, of which waited for: 8 -> 0; matrix products, arithmetic and copies ran while one was open for 8% -> 0% of each run, Pallas kernels for 0% -> 0%
where the time goes in v3:
time: 150 us; the launch traced here: 149 us
  Pallas kernels  145 us (97%)
  local copies, waits for them, and re-layouts  3.31 us (2%)
    pallas_call x1, Pallas kernels, on_device(): pl.pallas_call(whole_kernel, out_shape=(jax.ShapeDtypeStruct((panel_rows,...  145 us
    unnamed x2, local copies, waits for them, and re-layouts  3.31 us

profile of v3, /device:TPU:24, one launch (start us, length us, event | category | flops | bytes accessed | tf_op | source)
XLA Modules:
  0.0 148.6 jit_solution(791554059516857775)
XLA Ops:
  0.6 144.7 %whole.1 = (bf16[32,5120]{1,0:T(8,128)(2,1)}, bf16[128,640]{1,0:T(8,128)(2,1)}) custom-call(bf16[32,5120]{1,0:T(8,128)(2,1)} %x_ref.1, bf16[3,5120,640]{2,1,0:T(8,128)(2,1)} %w_hbm.1, bf16[128,640]{1,0:T(8,128)(2,1)} %readout_ref.1, s32[32,128]{1,0:T(8,128)} %bitcast.1, s32[8,8]{1,0:T(8,128)} %mask_ref.1), custom_call_target="tpu_custom_call" | custom-call | tf_op jit(solution)/shard_map/whole/pallas_call | solution.py:776
  145.3 1.7 %copy.9 = bf16[32,5120]{1,0:T(8,128)(2,1)} copy(bf16[32,5120]{1,0:T(8,128)(2,1)} %get-tuple-element.4) | data formatting | bytes 655360
  147.0 1.6 %copy.10 = bf16[128,640]{1,0:T(8,128)(2,1)} copy(bf16[128,640]{1,0:T(8,128)(2,1)} %get-tuple-element.5) | data formatting | bytes 327680

commit v4 on v3

--- a/solution.py
+++ b/solution.py
@@ -34,6 +34,7 @@
 
 
 PANELS = 10
+AHEAD = 4
 LAYERS = 4
 
 
@@ -422,7 +423,7 @@
     w_ref, x_all, gx_all, totals, q_heads, kv_heads, r_heads, qd_heads, kvd_heads,
     kv, dots, q, r, qd, key_hot, row_bar, barred, stat,
     dkv, dq_acc, dq, penalty, other, summed, landed, q_landed, p_landed, plain, grads,
-    parts, via, direct, mixed, mix_out,
+    parts, via, direct, mixed, mix_out, kept,
     w_sems, *sems
 ):
     sems = list(sems)
@@ -443,8 +444,7 @@
     for h in range(HEADS):
         r_heads[h] = readout_ref[:, h * HD : (h + 1) * HD]
     enter(chip, core, layers=True)
-    ahead = 3
-    for panel in range(ahead):
+    for panel in range(PANELS):
         gather.start(panel)
     r_begin, r_arrived, r_sent = deal_queries(chip, core, r_heads, r, *take(2))
     q_begin, q_arrived, q_sent = deal_queries(chip, core, q_heads, q, *take(2))
@@ -452,12 +452,11 @@
     r_begin()
     mask_sides(frames_ref, mask_ref, key_hot, row_bar, barred, first, core)
 
-    gather.relay(0)
+    for panel in range(AHEAD):
+        gather.relay(panel)
     for panel in range(PANELS):
-        if panel + ahead < PANELS:
-            gather.start(panel + ahead)
-        if panel + 1 < PANELS:
-            gather.relay(panel + 1)
+        if panel + AHEAD < PANELS:
+            gather.relay(panel + AHEAD)
         gather.rest(panel)
         panel_of_w(w_hbm, w_ref, w_sems, panel).wait()
         add_panel(totals, x_all, w_ref, panel, panel == 0)
@@ -521,10 +520,12 @@
     def key_grads(step):
         target = (chip + step) % CHIPS
         weights = jnp.exp2(logits(target) * FACTOR - stat[NORM])
+        weights_low = weights.astype(jnp.bfloat16)
+        kept[target] = weights_low
         readout_dots = nt(keys_of(kv.at[1], target), flat(r))
         slopes = (weights * (readout_dots - stat[ROW_DOTS])).astype(jnp.bfloat16)
         key_part = (SCALE * nn(slopes, flat(q))).astype(jnp.bfloat16)
-        value_part = nn(weights.astype(jnp.bfloat16), flat(r)).astype(jnp.bfloat16)
+        value_part = nn(weights_low, flat(r)).astype(jnp.bfloat16)
         dkv[0, target] = key_part.reshape(2, HD, HD)
         dkv[1, target] = value_part.reshape(2, HD, HD)
         swap(target).start()
@@ -557,10 +558,14 @@
             return carry
 
         lax.fori_loop(1, CHIPS, go, 0)
+        dq[...] = (SCALE * dq_acc[...]).T.astype(jnp.bfloat16).reshape(SLOTS, HD, HD)
+
+    dq_begin()
+
+    @pl.when(busy)
+    def _():
         add_partner(CHIPS - 1)
-        dq[...] = (SCALE * dq_acc[...]).T.astype(jnp.bfloat16).reshape(SLOTS, HD, HD)
-
-    dq_begin()
+
     gather.sent()
     kv_sent()
     q_sent()
@@ -656,8 +661,8 @@
         regather.rest(panel)
         add_panel(totals, gx_all, w_ref, panel, panel == 0)
 
-    stages = ((share, 0), (mix, 1), (settle, 3), (regather.relay, 4), (absorb, 6))
-    for step in range(PANELS + 6):
+    stages = ((share, 0), (mix, 3), (settle, 6), (regather.relay, 9), (absorb, 12))
+    for step in range(PANELS + stages[-1][1]):
         for stage, lag in stages:
             if 0 <= step - lag < PANELS:
                 stage(step - lag)
@@ -668,11 +673,11 @@
     def tangent(source):
         keys, values = keys_of(kv.at[0], source), keys_of(kv.at[1], source)
         key_dots, value_dots = keys_of(dots.at[0], source), keys_of(dots.at[1], source)
-        weights = jnp.exp2(logits(source) * FACTOR - stat[NORM])
+        weights_low = kept[source]
         moved = nt(jnp.concatenate([keys, key_dots], axis=1), jnp.concatenate([flat(qd), flat(q)], axis=1))
-        turned = weights * (moved * SCALE)
+        turned = weights_low.astype(jnp.float32) * (moved * SCALE)
         dq_acc[...] += tn(values, turned.astype(jnp.bfloat16))
-        plain[...] += tn(jnp.concatenate([values, value_dots], axis=1), weights.astype(jnp.bfloat16))
+        plain[...] += tn(jnp.concatenate([values, value_dots], axis=1), weights_low)
         stat[CURVE] += turned.sum(axis=0, keepdims=True)
 
     qd_arrived()
@@ -767,6 +772,7 @@
         direct=low(panel_rows, width),
         mixed=low(panel_rows, width),
         mix_out=low(panel_rows, width),
+        kept=low(CHIPS, CHUNK, ROWS),
         w_sems=DMA((PANELS,)),
     )
     sems = (

time: 150 us -> 137 us (0.913)
  Pallas kernels: 145 us -> 132 us
    pallas_call x1, Pallas kernels: 145 us -> 132 us  [on_device(): pl.pallas_call(whole_kernel, out_shape=(jax.ShapeDtypeStruct((panel_rows,...]
where the time goes in v4:
time: 137 us; the launch traced here: 136 us
  Pallas kernels  132 us (96%)
  local copies, waits for them, and re-layouts  3.31 us (2%)
    pallas_call x1, Pallas kernels, on_device(): pl.pallas_call(whole_kernel, out_shape=(jax.ShapeDtypeStruct((panel_rows,...  132 us
    unnamed x2, local copies, waits for them, and re-layouts  3.31 us

profile of v4, /device:TPU:24, one launch (start us, length us, event | category | flops | bytes accessed | tf_op | source)
XLA Modules:
  0.0 135.9 jit_solution(12063087004821939375)
XLA Ops:
  0.6 131.9 %whole.1 = (bf16[32,5120]{1,0:T(8,128)(2,1)}, bf16[128,640]{1,0:T(8,128)(2,1)}) custom-call(bf16[32,5120]{1,0:T(8,128)(2,1)} %x_ref.1, bf16[3,5120,640]{2,1,0:T(8,128)(2,1)} %w_hbm.1, bf16[128,640]{1,0:T(8,128)(2,1)} %readout_ref.1, s32[32,128]{1,0:T(8,128)} %bitcast.1, s32[8,8]{1,0:T(8,128)} %mask_ref.1), custom_call_target="tpu_custom_call" | custom-call | tf_op jit(solution)/shard_map/whole/pallas_call | solution.py:782
  132.5 1.7 %copy.9 = bf16[32,5120]{1,0:T(8,128)(2,1)} copy(bf16[32,5120]{1,0:T(8,128)(2,1)} %get-tuple-element.4) | data formatting | bytes 655360
  134.3 1.6 %copy.10 = bf16[128,640]{1,0:T(8,128)(2,1)} copy(bf16[128,640]{1,0:T(8,128)(2,1)} %get-tuple-element.5) | data formatting | bytes 327680

commit v5 on v4

--- a/solution.py
+++ b/solution.py
@@ -33,8 +33,8 @@
     return me // 2, me % 2
 
 
-PANELS = 10
-AHEAD = 4
+PANELS = 5
+AHEAD = 2
 LAYERS = 4
 
 
@@ -661,7 +661,7 @@
         regather.rest(panel)
         add_panel(totals, gx_all, w_ref, panel, panel == 0)
 
-    stages = ((share, 0), (mix, 3), (settle, 6), (regather.relay, 9), (absorb, 12))
+    stages = ((share, 0), (mix, 2), (settle, 4), (regather.relay, 6), (absorb, 8))
     for step in range(PANELS + stages[-1][1]):
         for stage, lag in stages:
             if 0 <= step - lag < PANELS:
@@ -721,6 +721,21 @@
     pen_end()
     for h in range(HEADS):
         pen_ref[:, h * HD : (h + 1) * HD] = p_landed[h]
+
+
+def hand_over_kernel(x_ref, p_ref, x_out, p_out):
+    x_out[...] = x_ref[...]
+    p_out[...] = p_ref[...]
+
+
+def hand_over(grad_x, penalty_grad):
+    return pl.pallas_call(
+        hand_over_kernel,
+        out_shape=tuple(jax.ShapeDtypeStruct(a.shape, a.dtype) for a in (grad_x, penalty_grad)),
+        in_specs=[VMEM] * 2,
+        out_specs=(VMEM, VMEM),
+        name="hand_over",
+    )(grad_x, penalty_grad)
 
 
 def on_device(clip_tokens, w_qkv, readout, token_latent_frame, frame_mask):
@@ -779,7 +794,7 @@
         gather_sems + query_sems * 2 + chip_sems + chip_sems + back_sems
         + gather_sems + query_sems + chip_sems + [DMA((PANELS,))] * 6 + back_sems
     )
-    return pl.pallas_call(
+    grad_x, penalty_grad = pl.pallas_call(
         whole_kernel,
         out_shape=(
             jax.ShapeDtypeStruct((panel_rows, width), jnp.bfloat16),
@@ -793,6 +808,7 @@
         ),
         name="whole",
     )(clip_tokens, w_qkv, readout, token_latent_frame.reshape(-1, HD), frame_mask)
+    return hand_over(grad_x, penalty_grad)
 
 
 def solution(mesh):

time: 137 us -> 135 us (0.985)
  local copies, waits for them, and re-layouts: 3.31 us -> 0 us
    unnamed x2 -> x0, local copies, waits for them, and re-layouts: 3.31 us -> none
    pallas_call x0 -> x1, Pallas kernels: none -> 1.81 us  [hand_over(): pl.pallas_call(hand_over_kernel, out_shape=tuple((jax.ShapeDtypeStruct(a....]
where the time goes in v5:
time: 135 us; the launch traced here: 133 us
  Pallas kernels  133 us (99%)
    pallas_call x1, Pallas kernels, on_device(): pl.pallas_call(whole_kernel, out_shape=(jax.ShapeDtypeStruct((panel_rows,...  131 us

profile of v5, /device:TPU:24, one launch (start us, length us, event | category | flops | bytes accessed | tf_op | source)
XLA Modules:
  0.0 133.3 jit_solution(108323126390705267)
XLA Ops:
  0.6 130.8 %whole.1 = (bf16[32,5120]{1,0:T(8,128)(2,1)}, bf16[128,640]{1,0:T(8,128)(2,1)}) custom-call(bf16[32,5120]{1,0:T(8,128)(2,1)} %x_ref.1, bf16[3,5120,640]{2,1,0:T(8,128)(2,1)} %w_hbm.1, bf16[128,640]{1,0:T(8,128)(2,1)} %readout_ref.1, s32[32,128]{1,0:T(8,128)} %bitcast.1, s32[8,8]{1,0:T(8,128)} %mask_ref.1), custom_call_target="tpu_custom_call" | custom-call | tf_op jit(solution)/shard_map/whole/pallas_call | solution.py:797
  131.5 1.8 %hand_over.1 = (bf16[32,5120]{1,0:T(8,128)(2,1)}, bf16[128,640]{1,0:T(8,128)(2,1)}) custom-call(bf16[32,5120]{1,0:T(8,128)(2,1)} %get-tuple-element.4.x_ref, bf16[128,640]{1,0:T(8,128)(2,1)} %get-tuple-element.5.p_ref), custom_call_target="tpu_custom_call" | custom-call | tf_op jit(solution)/shard_map/hand_over/pallas_call | solution.py:732

commit v6 on v5

--- a/solution.py
+++ b/solution.py
@@ -34,7 +34,7 @@
 
 
 PANELS = 5
-AHEAD = 2
+AHEAD = 4
 LAYERS = 4
 
 

time: 135 us -> 134 us (level)
  no operation moved by 1% of the time
where the time goes in v6:
time: 134 us; the launch traced here: 133 us
  Pallas kernels  133 us (99%)
    pallas_call x1, Pallas kernels, on_device(): pl.pallas_call(whole_kernel, out_shape=(jax.ShapeDtypeStruct((panel_rows,...  131 us

profile of v6, /device:TPU:24, one launch (start us, length us, event | category | flops | bytes accessed | tf_op | source)
XLA Modules:
  0.0 133.2 jit_solution(8915440083624890171)
XLA Ops:
  0.6 130.7 %whole.1 = (bf16[32,5120]{1,0:T(8,128)(2,1)}, bf16[128,640]{1,0:T(8,128)(2,1)}) custom-call(bf16[32,5120]{1,0:T(8,128)(2,1)} %x_ref.1, bf16[3,5120,640]{2,1,0:T(8,128)(2,1)} %w_hbm.1, bf16[128,640]{1,0:T(8,128)(2,1)} %readout_ref.1, s32[32,128]{1,0:T(8,128)} %bitcast.1, s32[8,8]{1,0:T(8,128)} %mask_ref.1), custom_call_target="tpu_custom_call" | custom-call | tf_op jit(solution)/shard_map/whole/pallas_call | solution.py:797
  131.4 1.8 %hand_over.1 = (bf16[32,5120]{1,0:T(8,128)(2,1)}, bf16[128,640]{1,0:T(8,128)(2,1)}) custom-call(bf16[32,5120]{1,0:T(8,128)(2,1)} %get-tuple-element.4.x_ref, bf16[128,640]{1,0:T(8,128)(2,1)} %get-tuple-element.5.p_ref), custom_call_target="tpu_custom_call" | custom-call | tf_op jit(solution)/shard_map/hand_over/pallas_call | solution.py:732
